TPU v7x, 32 devices: a whole 2x2x4 slice. The times are simulated.
32 devices in a mesh: judge: 2 (over y), gx: 4 (over z), gy: 2 (over core), gz: 2 (over x).
Axes of the slice: x: 2, y: 2, z: 4, core: 2. Of those that a mesh axis runs over, the one named last changes fastest.
Arguments:
- tokens: bfloat16 [2048, 8192], P(('judge', 'gy'), ('gz', 'gx')), parts along dimension 0, may hold values from -6 to 6
- out_grad: bfloat16 [2048, 8192], P(('judge', 'gy'), ('gz', 'gx')), parts along dimension 0, may hold values from -6 to 6
- gate_weight: bfloat16 [8192, 14336], P(('gz', 'gy'), 'gx'), may hold values from -0.09375 to 0.09375
- up_weight: bfloat16 [8192, 14336], P(('gz', 'gy'), 'gx'), may hold values from -0.0625 to 0.0625
- down_weight: bfloat16 [14336, 8192], P('gx', ('gz', 'gy')), may hold values from -0.046875 to 0.046875
Outputs:
- input_grad: bfloat16 [2048, 8192], P(('judge', 'gy'), ('gz', 'gx')), parts along dimension 0
- gate_grad: bfloat16 [16384, 14336], P(('judge', 'gz', 'gy'), 'gx'), parts along dimension 0
- up_grad: bfloat16 [16384, 14336], P(('judge', 'gz', 'gy'), 'gx'), parts along dimension 0
There are 2 independent parts, one for each index of `judge`. A program takes and returns all parts, laid end to end along the dimension named above; an argument that names none is the same for every part. Nothing has to cross between parts.
All inputs are finite; a program needn't handle non-finite values.
Results may differ from a plain program's by a relative error of at most 0.0051.
Values may be sent and summed in bfloat16 or wider, within the bound.
A program may use at most 384 MiB of HBM per device.

v0:
```python
import jax
import jax.numpy as jnp
from jax import lax
from jax.sharding import PartitionSpec as P


def swiglu_back(gate_sum, up_sum, back_sum):
    sigmoid_gate = jax.nn.sigmoid(gate_sum)
    grad_up = (back_sum * gate_sum * sigmoid_gate).astype(jnp.bfloat16)
    grad_gate = (back_sum * up_sum * sigmoid_gate * (1.0 + gate_sum * (1.0 - sigmoid_gate))).astype(
        jnp.bfloat16
    )
    return (grad_gate, grad_up)


def contract_last(left, right):
    return lax.dot_general(
        left, right, (((1,), (1,)), ((), ())), preferred_element_type=jnp.float32
    )


def contract_first(left, right):
    return lax.dot_general(
        left, right, (((0,), (0,)), ((), ())), preferred_element_type=jnp.float32
    )


def per_device(tokens, out_grad, gate_weight, up_weight, down_weight):
    weight_scale = float(tokens.shape[0] * lax.axis_size("gy")) ** (-0.5)
    feat_block, grad_block = (
        lax.all_gather(tokens, "gx", axis=1, tiled=True),
        lax.all_gather(out_grad, "gx", axis=1, tiled=True),
    )
    gate_block, up_block, down_block = (
        lax.all_gather(gate_weight, "gy", axis=0, tiled=True),
        lax.all_gather(up_weight, "gy", axis=0, tiled=True),
        lax.all_gather(down_weight, "gy", axis=1, tiled=True),
    )
    gate_part = jnp.dot(feat_block, gate_block, preferred_element_type=jnp.float32)
    up_part = jnp.dot(feat_block, up_block, preferred_element_type=jnp.float32)
    back_part = contract_last(grad_block, down_block)
    gate_sum, up_sum, back_sum = lax.psum((gate_part, up_part, back_part), "gz")
    grad_gate, grad_up = swiglu_back(gate_sum, up_sum, back_sum)
    input_part = contract_last(grad_gate, gate_block) + contract_last(grad_up, up_block)
    half_width = gate_weight.shape[0]
    row_offset = lax.axis_index("gy") * half_width
    features = lax.dynamic_slice_in_dim(
        lax.all_gather(feat_block, "gy", axis=0, tiled=True), row_offset, half_width, 1
    )
    gate_total = contract_first(features, lax.all_gather(grad_gate, "gy", axis=0, tiled=True))
    up_total = contract_first(features, lax.all_gather(grad_up, "gy", axis=0, tiled=True))
    input_grad = lax.psum_scatter(input_part, "gx", scatter_dimension=1, tiled=True).astype(
        jnp.bfloat16
    )
    gate_grad = (gate_total * weight_scale).astype(jnp.bfloat16)
    up_grad = (up_total * weight_scale).astype(jnp.bfloat16)
    return (input_grad, gate_grad, up_grad)


def solution(mesh):
    return jax.shard_map(
        per_device,
        mesh=mesh,
        in_specs=(
            P(("judge", "gy"), ("gz", "gx")),
            P(("judge", "gy"), ("gz", "gx")),
            P(("gz", "gy"), "gx"),
            P(("gz", "gy"), "gx"),
            P("gx", ("gz", "gy")),
        ),
        out_specs=(
            P(("judge", "gy"), ("gz", "gx")),
            P(("judge", "gz", "gy"), "gx"),
            P(("judge", "gz", "gy"), "gx"),
        ),
        check_vma=False,
    )
```

profile of v0, /device:TPU:0, one launch (start us, length us, event | category | flops | bytes accessed | tf_op | source)
XLA Modules:
  0.0 1059.5 jit_solution(10605519873700182976)
XLA Ops:
  7.2 0.0 all-gather.13.cloned.1.call-start
  7.2 0.7 all-gather.13.cloned.1.call-update
  7.9 0.0 all-gather.17.cloned.1.call-start
  7.9 0.7 all-gather.17.cloned.1.call-update
  8.6 0.0 all-gather.15.cloned.1.call-start
  8.7 0.7 all-gather.15.cloned.1.call-update
  9.4 0.0 all-gather.9.cloned.1.call-start
  9.4 0.5 all-gather.9.cloned.1.call-update
  10.0 0.0 all-gather.11.cloned.1.call-start
  10.0 0.5 all-gather.11.cloned.1.call-update
  10.5 0.0 all-reduce.3.cloned.1.call-start
  10.6 82.5 %all-gather.13.cloned.1.call-done = bf16[512,4096]{1,0:T(8,128)(2,1)} async-done(((bf16[512,1024]{1,0:T(8,128)(2,1)}), bf16[512,4096]{1,0:T(8,128)(2,1)}) %all-gather.13.cloned.1.call-update) | async-done | bytes 4194320 | tf_op jit(solution)/shard_map/all_gather | solution.py:31
  93.1 47.0 %all-gather.17.cloned.1.call-done = bf16[4096,3584]{1,0:T(8,128)(2,1)} async-done(((bf16[2048,3584]{1,0:T(8,128)(2,1)}), bf16[4096,3584]{1,0:T(8,128)(2,1)}) %all-gather.17.cloned.1.call-update) | async-done | bytes 29360144 | tf_op jit(solution)/shard_map/all_gather | solution.py:35
  140.0 24.2 %fusion.6 = f32[512,3584]{1,0:T(8,128)} fusion(bf16[512,4096]{1,0:T(8,128)(2,1)} %all-gather.13.cloned.1.call-done, bf16[4096,3584]{1,0:T(8,128)(2,1)} %all-gather.17.cloned.1.call-done), kind=kOutput, calls=%fused_computation.12 | convolution fusion | flops 15032385536 | bytes 40894464 | tf_op jit(solution)/shard_map/dot_general | solution.py:39
  164.2 25.4 %all-gather.15.cloned.1.call-done = bf16[4096,3584]{1,0:T(8,128)(2,1)} async-done(((bf16[2048,3584]{1,0:T(8,128)(2,1)}), bf16[4096,3584]{1,0:T(8,128)(2,1)}) %all-gather.15.cloned.1.call-update) | async-done | bytes 29360144 | tf_op jit(solution)/shard_map/all_gather | solution.py:36
  189.6 24.0 %fusion.5 = f32[512,3584]{1,0:T(8,128)} fusion(bf16[512,4096]{1,0:T(8,128)(2,1)} %all-gather.13.cloned.1.call-done, bf16[4096,3584]{1,0:T(8,128)(2,1)} %all-gather.15.cloned.1.call-done), kind=kOutput, calls=%fused_computation.11 | convolution fusion | flops 15032385536 | bytes 40894464 | tf_op jit(solution)/shard_map/dot_general | solution.py:40
  213.6 59.4 %all-gather.9.cloned.1.call-done = bf16[512,4096]{1,0:T(8,128)(2,1)} async-done(((bf16[512,1024]{1,0:T(8,128)(2,1)}), bf16[512,4096]{1,0:T(8,128)(2,1)}) %all-gather.9.cloned.1.call-update) | async-done | bytes 4194320 | tf_op jit(solution)/shard_map/all_gather | solution.py:32
  273.0 46.8 %all-gather.11.cloned.1.call-done = bf16[3584,4096]{1,0:T(8,128)(2,1)} async-done(((bf16[3584,2048]{1,0:T(8,128)(2,1)}), bf16[3584,4096]{1,0:T(8,128)(2,1)}) %all-gather.11.cloned.1.call-update) | async-done | bytes 29360144 | tf_op jit(solution)/shard_map/all_gather | solution.py:37
  319.8 23.9 %fusion.4 = f32[512,3584]{1,0:T(8,128)} fusion(bf16[512,4096]{1,0:T(8,128)(2,1)} %all-gather.9.cloned.1.call-done, bf16[3584,4096]{1,0:T(8,128)(2,1)} %all-gather.11.cloned.1.call-done), kind=kOutput, calls=%fused_computation.10 | convolution fusion | flops 15032385536 | bytes 40894464 | tf_op jit(solution)/shard_map/dot_general | solution.py:17
  343.7 0.0 all-reduce.3.cloned.1.call-update
  343.8 0.0 all-gather.19.cloned.1.call-start
  343.8 0.7 all-gather.19.cloned.1.call-update
  344.5 0.0 all-gather.21.cloned.1.call-start
  344.6 493.1 %all-reduce.3.cloned.1.call-done = (f32[512,3584]{1,0:T(8,128)}, f32[512,3584]{1,0:T(8,128)}, f32[512,3584]{1,0:T(8,128)}) async-done(((f32[512,3584]{1,0:T(8,128)}, f32[512,3584]{1,0:T(8,128)}, f32[512,3584]{1,0:T(8,128)}), (f32[512,3584]{1,0:T(8,128)}, f32[512,3584]{1,0:T(8,128)}, f32[512,3584]{1,0:T(8,128)})) %all-reduce.3.cloned.1.call-update) | async-done | bytes 22020112 | tf_op jit(solution)/shard_map/psum | solution.py:42
  837.7 11.4 %multiply_convert_fusion.2 = (bf16[512,3584]{1,0:T(8,128)(2,1)}, bf16[512,3584]{1,0:T(8,128)(2,1)}) fusion(f32[512,3584]{1,0:T(8,128)} %get-tuple-element.4, f32[512,3584]{1,0:T(8,128)} %get-tuple-element.3, f32[512,3584]{1,0:T(8,128)} %get-tuple-element.5), kind=kLoop, calls=%fused_computation.2 | loop fusion | flops 23855104 | bytes 29360128 | tf_op jit(solution)/shard_map/convert_element_type | solution.py:9
  849.1 0.0 all-gather.21.cloned.1.call-update
  849.1 0.0 all-gather.23.cloned.1.call-start
  849.2 0.7 all-gather.23.cloned.1.call-update
  849.9 0.0 reduce-scatter.2.cloned.1.call-start
  849.9 23.5 %fusion.7 = f32[512,4096]{1,0:T(8,128)} fusion(bf16[512,3584]{1,0:T(8,128)(2,1)} %get-tuple-element.7, bf16[4096,3584]{1,0:T(8,128)(2,1)} %all-gather.17.cloned.1.call-done), kind=kOutput, calls=%fused_computation.13 | convolution fusion | flops 15032385536 | bytes 41418752 | tf_op jit(solution)/shard_map/dot_general | solution.py:17
  873.5 27.4 %convolution_add_fusion = f32[512,4096]{1,0:T(8,128)} fusion(f32[512,4096]{1,0:T(8,128)} %fusion.7, bf16[512,3584]{1,0:T(8,128)(2,1)} %get-tuple-element.6, bf16[4096,3584]{1,0:T(8,128)(2,1)} %all-gather.15.cloned.1.call-done), kind=kOutput, calls=%fused_computation.5 | convolution fusion | flops 15034482688 | bytes 49807360 | tf_op jit(solution)/shard_map/dot_general | solution.py:17
  900.8 0.0 reduce-scatter.2.cloned.1.call-update
  900.9 0.0 all-gather.19.cloned.1.call-done
  900.9 0.0 all-gather.21.cloned.1.call-done
  900.9 22.4 %multiply_convert_fusion.1 = bf16[2048,3584]{1,0:T(8,128)(2,1)} fusion(bf16[1024,3584]{1,0:T(8,128)(2,1)} %all-gather.21.cloned.1.call-done, bf16[1024,4096]{1,0:T(8,128)(2,1)} %all-gather.19.cloned.1.call-done, s32[]{:T(128)S(6)} %select_n.3), kind=kOutput, calls=%fused_computation.1 | convolution fusion | flops 15047065600 | bytes 26214404 | tf_op jit(solution)/shard_map/dot_general | solution.py:23
  923.3 0.0 all-gather.23.cloned.1.call-done
  923.3 22.5 %multiply_convert_fusion = bf16[2048,3584]{1,0:T(8,128)(2,1)} fusion(bf16[1024,3584]{1,0:T(8,128)(2,1)} %all-gather.23.cloned.1.call-done, bf16[1024,4096]{1,0:T(8,128)(2,1)} %all-gather.19.cloned.1.call-done, s32[]{:T(128)S(6)} %select_n.3), kind=kOutput, calls=%fused_computation | convolution fusion | flops 15047065600 | bytes 26214404 | tf_op jit(solution)/shard_map/dot_general | solution.py:23
  945.8 103.9 %reduce-scatter.2.cloned.1.call-done = f32[512,1024]{1,0:T(8,128)} async-done(((f32[512,4096]{1,0:T(8,128)}), f32[512,1024]{1,0:T(8,128)}) %reduce-scatter.2.cloned.1.call-update) | async-done | bytes 2097168 | tf_op jit(solution)/shard_map/reduce_scatter | solution.py:52
  1049.7 2.7 convert_element_type.17
Async XLA Ops:
  7.2 85.9 %all-gather.13.cloned.1.call-start = ((), (), s32[]{:S(2)}) async-start(), calls=%async_computation.3 | async-start | bytes 5242880 | tf_op jit(solution)/shard_map/all_gather | solution.py:31
  7.9 132.1 %all-gather.17.cloned.1.call-start = ((), (), s32[]{:S(2)}) async-start(), calls=%async_computation.5 | async-start | bytes 44040192 | tf_op jit(solution)/shard_map/all_gather | solution.py:35
  8.6 181.0 %all-gather.15.cloned.1.call-start = ((), (), s32[]{:S(2)}) async-start(), calls=%async_computation.4 | async-start | bytes 44040192 | tf_op jit(solution)/shard_map/all_gather | solution.py:36
  9.4 263.6 %all-gather.9.cloned.1.call-start = ((), (), s32[]{:S(2)}) async-start(), calls=%async_computation.1 | async-start | bytes 5242880 | tf_op jit(solution)/shard_map/all_gather | solution.py:32
  10.0 309.9 %all-gather.11.cloned.1.call-start = ((), (), s32[]{:S(2)}) async-start(), calls=%async_computation.2 | async-start | bytes 44040192 | tf_op jit(solution)/shard_map/all_gather | solution.py:37
  10.5 827.1 %all-reduce.3.cloned.1.call-start = ((), (), s32[]{:S(2)}) async-start(), calls=%async_computation.10 | async-start | bytes 44040192 | tf_op jit(solution)/shard_map/psum | solution.py:42
  343.8 557.1 %all-gather.19.cloned.1.call-start = ((), (), s32[]{:S(2)}) async-start(), calls=%async_computation.7 | async-start | bytes 12582912 | tf_op jit(solution)/shard_map/all_gather | solution.py:48
  344.5 556.4 %all-gather.21.cloned.1.call-start = ((), (), s32[]{:S(2)}) async-start(), calls=%async_computation.8 | async-start | bytes 11010048 | tf_op jit(solution)/shard_map/all_gather | solution.py:50
  849.1 74.2 %all-gather.23.cloned.1.call-start = ((), (), s32[]{:S(2)}) async-start(), calls=%async_computation.9 | async-start | bytes 11010048 | tf_op jit(solution)/shard_map/all_gather | solution.py:51
  849.9 199.8 %reduce-scatter.2.cloned.1.call-start = ((), (), s32[]{:S(2)}) async-start(), calls=%async_computation.6 | async-start | bytes 10485760 | tf_op jit(solution)/shard_map/reduce_scatter | solution.py:52
Sparse Core Ops, SparseCore 0:
  9.6 83.4 all-gather.12
  94.6 45.3 all-gather.16
  141.6 47.9 all-gather.14
  191.0 81.9 all-gather.8
  274.4 45.3 all-gather.10
  343.9 493.7 all-reduce.2
  839.2 19.8 all-gather.18
  861.2 19.4 all-gather.20
  882.3 19.4 all-gather.22
  904.0 145.6 reduce-scatter.1
where the time goes:
time: 1070 us; the launch traced here: 1060 us
  waiting for transfers between devices  863 us (81%)
  matrix products  168 us (16%)
  between operations  14.5 us (1%)
  other arithmetic  14.2 us (1%)
    psum x1, waiting for transfers between devices, per_device(): gate_sum, up_sum, back_sum = lax.psum((gate_part, up_part, back_part), 'gz')  493 us
    reduce_scatter x1, waiting for transfers between devices, per_device(): lax.psum_scatter(input_part, 'gx', scatter_dimension=1, tiled=True)  104 us
    all_gather x1, waiting for transfers between devices, per_device(): lax.all_gather(tokens, 'gx', axis=1, tiled=True)  82.5 us
    dot_general x3, matrix products, contract_last(): lax.dot_general(left, right, (((1,), (1,)), ((), ())), preferred_element_...  74.9 us
    all_gather x1, waiting for transfers between devices, per_device(): lax.all_gather(out_grad, 'gx', axis=1, tiled=True)  59.4 us
    all_gather x1, waiting for transfers between devices, per_device(): lax.all_gather(gate_weight, 'gy', axis=0, tiled=True)  47 us
    all_gather x1, waiting for transfers between devices, per_device(): lax.all_gather(down_weight, 'gy', axis=1, tiled=True)  46.8 us
    dot_general x2, matrix products, contract_first(): lax.dot_general(left, right, (((0,), (0,)), ((), ())), preferred_element_...  44.9 us
  transfers between devices with their start and end apart: 10, of which 7 were waited for; matrix products, arithmetic and copies ran while one was open for 15% of the time, Pallas kernels for 0%

commit v1 on v0

v1 whole, which is shorter than its diff:
```python
import jax
import jax.numpy as jnp
from jax import lax
from jax.sharding import PartitionSpec as P

CHUNKS = 4


def swiglu_back(gate_sum, up_sum, back_sum):
    sigmoid_gate = jax.nn.sigmoid(gate_sum)
    grad_up = (back_sum * gate_sum * sigmoid_gate).astype(jnp.bfloat16)
    grad_gate = (back_sum * up_sum * sigmoid_gate * (1.0 + gate_sum * (1.0 - sigmoid_gate))).astype(
        jnp.bfloat16
    )
    return (grad_gate, grad_up)


def contract_last(left, right):
    return lax.dot_general(
        left, right, (((1,), (1,)), ((), ())), preferred_element_type=jnp.float32
    )


def contract_first(left, right):
    return lax.dot_general(
        left, right, (((0,), (0,)), ((), ())), preferred_element_type=jnp.float32
    )


def shift(block, axis, step):
    count = lax.axis_size(axis)
    return lax.ppermute(block, axis, [(i, (i + step) % count) for i in range(count)])


def block_of(array, index, size, dim=0):
    return lax.dynamic_slice_in_dim(array, index * size, size, dim)


def scatter_sum(total, axis):
    count, me = lax.axis_size(axis), lax.axis_index(axis)
    size = total.shape[0] // count
    own = block_of(total, me, size)
    for step in range(1, count):
        away = block_of(total, lax.rem(me + step, count), size).astype(jnp.bfloat16)
        own = own + shift(away, axis, step).astype(jnp.float32)
    return own


def gather_rows(block, axis):
    count, me = lax.axis_size(axis), lax.axis_index(axis)
    size = block.shape[0]
    if count == 2:
        other = shift(block, axis, 1)
        first = me == 0
        return jnp.concatenate(
            [jnp.where(first, block, other), jnp.where(first, other, block)], axis=0
        )
    whole = jnp.zeros((count * size,) + block.shape[1:], block.dtype)
    whole = lax.dynamic_update_slice_in_dim(whole, block, me * size, 0)
    for step in range(1, count):
        got = shift(block, axis, step)
        source = lax.rem(me + count - step, count)
        whole = lax.dynamic_update_slice_in_dim(whole, got, source * size, 0)
    return whole


def per_device(tokens, out_grad, gate_weight, up_weight, down_weight):
    rows, shard = tokens.shape
    weight_scale = float(rows * lax.axis_size("gy")) ** (-0.5)
    width = gate_weight.shape[0]
    shards = width // shard
    gy = lax.axis_index("gy")
    chunk = rows // CHUNKS

    def load(index):
        pair = jnp.stack(
            [
                tokens[index * chunk : (index + 1) * chunk],
                out_grad[index * chunk : (index + 1) * chunk],
            ]
        )
        blocks = lax.all_gather(pair, "gx", axis=0)
        mine = block_of(blocks, gy, shards)
        other = shift(block_of(blocks, 1 - gy, shards), "gy", 1)
        both = jnp.concatenate([mine, other], axis=2)
        both = both.transpose(1, 2, 0, 3).reshape(2, 2 * chunk, width)
        return both[0], both[1]

    def core_sum(part):
        return part[:chunk] + shift(part[chunk:], "gy", 1)

    def sums(features, grads):
        out = []
        for left, weight, dot in (
            (features, gate_weight, lambda a, b: jnp.dot(a, b, preferred_element_type=jnp.float32)),
            (features, up_weight, lambda a, b: jnp.dot(a, b, preferred_element_type=jnp.float32)),
            (grads, down_weight, contract_last),
        ):
            out.append(scatter_sum(core_sum(dot(left, weight)), "gz"))
        return out

    def spread(grad):
        half = gather_rows(grad, "gz")
        return jnp.concatenate([half, shift(half, "gy", 1)], axis=0)

    def input_rows(grad_gate, grad_up):
        part = contract_last(grad_gate, gate_weight) + contract_last(grad_up, up_weight)
        part = part.astype(jnp.bfloat16)
        mine, other = part[:chunk], shift(part[chunk:], "gy", 1)
        first = gy == 0
        whole = jnp.concatenate(
            [jnp.where(first, mine, other), jnp.where(first, other, mine)], axis=1
        )
        count, me = lax.axis_size("gx"), lax.axis_index("gx")
        if count > 8:
            total = lax.psum_scatter(
                whole.astype(jnp.float32), "gx", scatter_dimension=1, tiled=True
            )
            return total.astype(jnp.bfloat16)
        total = block_of(whole, me, shard, 1).astype(jnp.float32)
        for step in range(1, count):
            away = block_of(whole, lax.rem(me + step, count), shard, 1)
            total = total + shift(away, "gx", step).astype(jnp.float32)
        return total.astype(jnp.bfloat16)

    features, gates, ups, inputs = [], [], [], []
    for index in range(CHUNKS):
        feature, grad = load(index)
        grad_gate, grad_up = swiglu_back(*sums(feature, grad))
        grad_gate, grad_up = spread(grad_gate), spread(grad_up)
        inputs.append(input_rows(grad_gate, grad_up))
        features.append(feature)
        gates.append(grad_gate)
        ups.append(grad_up)
    features = jnp.concatenate(features, axis=0)
    gate_total = contract_first(features, jnp.concatenate(gates, axis=0))
    up_total = contract_first(features, jnp.concatenate(ups, axis=0))
    gate_grad = (gate_total * weight_scale).astype(jnp.bfloat16)
    up_grad = (up_total * weight_scale).astype(jnp.bfloat16)
    return (jnp.concatenate(inputs, axis=0), gate_grad, up_grad)


def solution(mesh):
    return jax.shard_map(
        per_device,
        mesh=mesh,
        in_specs=(
            P(("judge", "gy"), ("gz", "gx")),
            P(("judge", "gy"), ("gz", "gx")),
            P(("gz", "gy"), "gx"),
            P(("gz", "gy"), "gx"),
            P("gx", ("gz", "gy")),
        ),
        out_specs=(
            P(("judge", "gy"), ("gz", "gx")),
            P(("judge", "gz", "gy"), "gx"),
            P(("judge", "gz", "gy"), "gx"),
        ),
        check_vma=False,
    )
```

time: 1070 us -> 817 us (0.76); the launches traced: 1060 us -> 818 us
  waiting for transfers between devices: 863 us -> 369 us
  matrix products: 168 us -> 247 us
  local copies, waits for them, and re-layouts: 0 us -> 77.6 us
  other arithmetic: 14.2 us -> 64.2 us
  starting transfers between devices: 0.39 us -> 46.1 us
    psum x1 -> x0, waiting for transfers between devices: 493 us -> none  [per_device(): gate_sum, up_sum, back_sum = lax.psum((gate_part, up_part, back_part), 'gz')]
    ppermute x0 -> x60, waiting for transfers between devices: none -> 191 us  [shift(): lax.ppermute(block, axis, [(i, (i + step) % count) for i in range(count)])]
    reduce_scatter x1 -> x0, waiting for transfers between devices: 104 us -> none  [per_device(): lax.psum_scatter(input_part, 'gx', scatter_dimension=1, tiled=True)]
    all_gather x8 -> x4, waiting for transfers between devices: 261 us -> 177 us  [load(): blocks = lax.all_gather(pair, 'gx', axis=0)]
    ppermute x0 -> x60, starting transfers between devices: none -> 45.9 us  [shift(): lax.ppermute(block, axis, [(i, (i + step) % count) for i in range(count)])]
    dot_general x3 -> x12, matrix products: 74.9 us -> 120 us  [contract_last(): lax.dot_general(left, right, (((1,), (1,)), ((), ())), preferred_element_...]
    dot_general x2 -> x8, matrix products: 48.2 us -> 85 us  [sums(): jnp.dot(a, b, preferred_element_type=jnp.float32)]
    slice x0 -> x28, local copies, waits for them, and re-layouts: none -> 35.9 us  [the longest x12 16.5 us: core_sum(): return part[:chunk] + shift(part[chunk:], 'gy', 1)]
  transfers between devices with their start and end apart: 10 -> 64, of which waited for: 7 -> 25; matrix products, arithmetic and copies ran while one was open for 15% -> 41% of each run, Pallas kernels for 0% -> 0%
where the time goes in v1:
time: 817 us; the launch traced here: 818 us
  waiting for transfers between devices  369 us (45%)
  matrix products  247 us (30%)
  local copies, waits for them, and re-layouts  77.6 us (9%)
  other arithmetic  64.2 us (8%)
  starting transfers between devices  46.1 us (6%)
  between operations  14.8 us (2%)
    ppermute x60, waiting for transfers between devices, shift(): lax.ppermute(block, axis, [(i, (i + step) % count) for i in range(count)])  191 us
    all_gather x4, waiting for transfers between devices, load(): blocks = lax.all_gather(pair, 'gx', axis=0)  177 us
    dot_general x12, matrix products, contract_last(): lax.dot_general(left, right, (((1,), (1,)), ((), ())), preferred_element_...  120 us
    dot_general x8, matrix products, sums(): jnp.dot(a, b, preferred_element_type=jnp.float32)  85 us
    ppermute x60, starting transfers between devices, shift(): lax.ppermute(block, axis, [(i, (i + step) % count) for i in range(count)])  45.9 us
    dot_general x2, matrix products, contract_first(): lax.dot_general(left, right, (((0,), (0,)), ((), ())), preferred_element_...  42 us
    unnamed x104, local copies, waits for them, and re-layouts  21 us
    unnamed x16, other arithmetic  19.6 us
  transfers between devices with their start and end apart: 64, of which 25 were waited for; matrix products, arithmetic and copies ran while one was open for 41% of the time, Pallas kernels for 0%

profile of v1, /device:TPU:0, one launch (start us, length us, event | category | flops | bytes accessed | tf_op | source)
XLA Modules:
  0.0 818.0 jit_solution(12613568808293119915)
XLA Ops:
  12.6 46.2 %all-gather.9.cloned.1.call-done = bf16[8,128,1024]{2,1,0:T(8,128)(2,1)} async-done(((bf16[2,128,1024]{2,1,0:T(8,128)(2,1)}), bf16[8,128,1024]{2,1,0:T(8,128)(2,1)}) %all-gather.9.cloned.1.call-update) | async-done | bytes 2097168 | tf_op jit(solution)/shard_map/all_gather | solution.py:82
  61.6 44.1 %all-gather.11.cloned.1.call-done = bf16[8,128,1024]{2,1,0:T(8,128)(2,1)} async-done(((bf16[2,128,1024]{2,1,0:T(8,128)(2,1)}), bf16[8,128,1024]{2,1,0:T(8,128)(2,1)}) %all-gather.11.cloned.1.call-update) | async-done | bytes 2097168 | tf_op jit(solution)/shard_map/all_gather | solution.py:82
  105.6 3.1 constant_dynamic-slice_fusion.5
  108.7 43.8 %all-gather.13.cloned.1.call-done = bf16[8,128,1024]{2,1,0:T(8,128)(2,1)} async-done(((bf16[2,128,1024]{2,1,0:T(8,128)(2,1)}), bf16[8,128,1024]{2,1,0:T(8,128)(2,1)}) %all-gather.13.cloned.1.call-update) | async-done | bytes 2097168 | tf_op jit(solution)/shard_map/all_gather | solution.py:82
  152.5 2.8 constant_dynamic-slice_fusion.3
  155.3 43.3 %all-gather.15.cloned.1.call-done = bf16[8,128,1024]{2,1,0:T(8,128)(2,1)} async-done(((bf16[2,128,1024]{2,1,0:T(8,128)(2,1)}), bf16[8,128,1024]{2,1,0:T(8,128)(2,1)}) %all-gather.15.cloned.1.call-update) | async-done | bytes 2097168 | tf_op jit(solution)/shard_map/all_gather | solution.py:82
  198.6 2.8 constant_dynamic-slice_fusion.1
  206.1 9.5 %fusion.79 = f32[256,3584]{1,0:T(8,128)} fusion(bf16[256,2048]{0,1:T(8,128)(2,1)S(1)} %bitcast.70, bf16[2048,3584]{1,0:T(8,128)(2,1)} %param.8), kind=kOutput, calls=%fused_computation.247 | convolution fusion | flops 3758096384 | bytes 19398656 | tf_op jit(solution)/shard_map/dot_general | solution.py:96
  215.6 9.2 %fusion.80 = f32[256,3584]{1,0:T(8,128)} fusion(bf16[256,2048]{0,1:T(8,128)(2,1)S(1)} %bitcast.71, bf16[2048,3584]{1,0:T(8,128)(2,1)} %param.7), kind=kOutput, calls=%fused_computation.248 | convolution fusion | flops 3758096384 | bytes 19398656 | tf_op jit(solution)/shard_map/dot_general | solution.py:95
  229.3 9.5 %fusion.82 = f32[256,3584]{1,0:T(8,128)} fusion(bf16[256,2048]{0,1:T(8,128)(2,1)S(1)} %bitcast.74, bf16[2048,3584]{1,0:T(8,128)(2,1)} %param.8), kind=kOutput, calls=%fused_computation.250 | convolution fusion | flops 3758096384 | bytes 19398656 | tf_op jit(solution)/shard_map/dot_general | solution.py:96
  238.8 9.1 %fusion.83 = f32[256,3584]{1,0:T(8,128)} fusion(bf16[256,2048]{0,1:T(8,128)(2,1)S(1)} %bitcast.75, bf16[2048,3584]{1,0:T(8,128)(2,1)} %param.7), kind=kOutput, calls=%fused_computation.251 | convolution fusion | flops 3758096384 | bytes 19398656 | tf_op jit(solution)/shard_map/dot_general | solution.py:95
  252.0 9.6 %fusion.85 = f32[256,3584]{1,0:T(8,128)} fusion(bf16[256,2048]{0,1:T(8,128)(2,1)S(1)} %bitcast.78, bf16[2048,3584]{1,0:T(8,128)(2,1)} %param.8), kind=kOutput, calls=%fused_computation.253 | convolution fusion | flops 3758096384 | bytes 19398656 | tf_op jit(solution)/shard_map/dot_general | solution.py:96
  261.6 19.2 %fusion.86 = f32[256,3584]{1,0:T(8,128)} fusion(bf16[256,2048]{0,1:T(8,128)(2,1)S(1)} %bitcast.79, bf16[2048,3584]{1,0:T(8,128)(2,1)} %param.7), kind=kOutput, calls=%fused_computation.254 | convolution fusion | flops 3758096384 | bytes 19398656 | tf_op jit(solution)/shard_map/dot_general | solution.py:95
  284.8 9.6 %fusion.88 = f32[256,3584]{1,0:T(8,128)} fusion(bf16[256,2048]{0,1:T(8,128)(2,1)S(1)} %bitcast.82, bf16[2048,3584]{1,0:T(8,128)(2,1)} %param.8), kind=kOutput, calls=%fused_computation.256 | convolution fusion | flops 3758096384 | bytes 19398656 | tf_op jit(solution)/shard_map/dot_general | solution.py:96
  294.4 9.2 %fusion.89 = f32[256,3584]{1,0:T(8,128)} fusion(bf16[256,2048]{0,1:T(8,128)(2,1)S(1)} %bitcast.83, bf16[2048,3584]{1,0:T(8,128)(2,1)} %param.7), kind=kOutput, calls=%fused_computation.257 | convolution fusion | flops 3758096384 | bytes 19398656 | tf_op jit(solution)/shard_map/dot_general | solution.py:95
  306.8 7.6 fusion.78
  323.1 7.6 fusion.81
  336.1 9.2 %fusion.84 = f32[256,3584]{1,0:T(8,128)} fusion(bf16[256,2048]{0,1:T(8,128)(2,1)S(1)} %bitcast.90, bf16[3584,2048]{1,0:T(8,128)(2,1)} %param.9), kind=kOutput, calls=%fused_computation.252 | convolution fusion | flops 3758096384 | bytes 19398656 | tf_op jit(solution)/shard_map/dot_general | solution.py:19
  345.3 8.2 fusion.87
  398.3 8.4 %collective-permute-done.2 = bf16[64,3584]{1,0:T(8,128)(2,1)S(1)} collective-permute-done((bf16[64,3584]{1,0:T(8,128)(2,1)S(1)}, bf16[64,3584]{1,0:T(8,128)(2,1)S(1)}, u32[]{:S(2)}, u32[]{:S(2)}) %collective-permute-start.2) | collective-permute-done | bytes 458784 | tf_op jit(solution)/shard_map/ppermute | solution.py:32
  408.2 8.4 %collective-permute-done.6 = bf16[64,3584]{1,0:T(8,128)(2,1)S(1)} collective-permute-done((bf16[64,3584]{1,0:T(8,128)(2,1)S(1)}, bf16[64,3584]{1,0:T(8,128)(2,1)S(1)}, u32[]{:S(2)}, u32[]{:S(2)}) %collective-permute-start.6) | collective-permute-done | bytes 458784 | tf_op jit(solution)/shard_map/ppermute | solution.py:32
  418.6 7.8 collective-permute-done.19
  427.8 8.4 %collective-permute-done.17 = bf16[64,3584]{1,0:T(8,128)(2,1)S(1)} collective-permute-done((bf16[64,3584]{1,0:T(8,128)(2,1)S(1)}, bf16[64,3584]{1,0:T(8,128)(2,1)S(1)}, u32[]{:S(2)}, u32[]{:S(2)}) %collective-permute-start.17) | collective-permute-done | bytes 458784 | tf_op jit(solution)/shard_map/ppermute | solution.py:32
  437.7 8.4 %collective-permute-done.21 = bf16[64,3584]{1,0:T(8,128)(2,1)S(1)} collective-permute-done((bf16[64,3584]{1,0:T(8,128)(2,1)S(1)}, bf16[64,3584]{1,0:T(8,128)(2,1)S(1)}, u32[]{:S(2)}, u32[]{:S(2)}) %collective-permute-start.21) | collective-permute-done | bytes 458784 | tf_op jit(solution)/shard_map/ppermute | solution.py:32
  448.1 7.8 collective-permute-done.34
  457.3 8.4 %collective-permute-done.32 = bf16[64,3584]{1,0:T(8,128)(2,1)S(1)} collective-permute-done((bf16[64,3584]{1,0:T(8,128)(2,1)S(1)}, bf16[64,3584]{1,0:T(8,128)(2,1)S(1)}, u32[]{:S(2)}, u32[]{:S(2)}) %collective-permute-start.32) | collective-permute-done | bytes 458784 | tf_op jit(solution)/shard_map/ppermute | solution.py:32
  467.1 8.4 %collective-permute-done.36 = bf16[64,3584]{1,0:T(8,128)(2,1)S(1)} collective-permute-done((bf16[64,3584]{1,0:T(8,128)(2,1)S(1)}, bf16[64,3584]{1,0:T(8,128)(2,1)S(1)}, u32[]{:S(2)}, u32[]{:S(2)}) %collective-permute-start.36) | collective-permute-done | bytes 458784 | tf_op jit(solution)/shard_map/ppermute | solution.py:32
  477.6 7.8 collective-permute-done.49
  486.8 8.4 %collective-permute-done.47 = bf16[64,3584]{1,0:T(8,128)(2,1)S(1)} collective-permute-done((bf16[64,3584]{1,0:T(8,128)(2,1)S(1)}, bf16[64,3584]{1,0:T(8,128)(2,1)S(1)}, u32[]{:S(2)}, u32[]{:S(2)}) %collective-permute-start.47) | collective-permute-done | bytes 458784 | tf_op jit(solution)/shard_map/ppermute | solution.py:32
  496.6 8.4 %collective-permute-done.51 = bf16[64,3584]{1,0:T(8,128)(2,1)S(1)} collective-permute-done((bf16[64,3584]{1,0:T(8,128)(2,1)S(1)}, bf16[64,3584]{1,0:T(8,128)(2,1)S(1)}, u32[]{:S(2)}, u32[]{:S(2)}) %collective-permute-start.51) | collective-permute-done | bytes 458784 | tf_op jit(solution)/shard_map/ppermute | solution.py:32
  507.1 7.8 collective-permute-done.9
  516.8 27.6 %collective-permute-done.7 = bf16[64,3584]{1,0:T(8,128)(2,1)S(1)} collective-permute-done((bf16[64,3584]{1,0:T(8,128)(2,1)S(1)}, bf16[64,3584]{1,0:T(8,128)(2,1)S(1)}, u32[]{:S(2)}, u32[]{:S(2)}) %collective-permute-start.7) | collective-permute-done | bytes 458784 | tf_op jit(solution)/shard_map/ppermute | solution.py:32
  551.6 11.0 %fusion.9 = f32[256,2048]{1,0:T(8,128)} fusion(bf16[2048,3584]{1,0:T(8,128)(2,1)} %param.8, bf16[128,3584]{1,0:T(8,128)(2,1)} %copy-done.45, bf16[64,3584]{1,0:T(8,128)(2,1)S(1)} %get-tuple-element.16, bf16[64,3584]{1,0:T(8,128)(2,1)S(1)} %get-tuple-element.18), kind=kOutput, calls=%fused_computation.32 | convolution fusion | flops 3763601408 | bytes 18612224 | tf_op jit(solution)/shard_map/dot_general | solution.py:19
  562.6 11.3 %fusion = bf16[256,2048]{1,0:T(8,128)(2,1)} fusion(f32[256,2048]{1,0:T(8,128)} %fusion.9, bf16[2048,3584]{1,0:T(8,128)(2,1)} %param.7, bf16[128,3584]{1,0:T(8,128)(2,1)} %collective-permute-done.8, bf16[64,3584]{1,0:T(8,128)(2,1)} %copy-done.39, bf16[64,3584]{1,0:T(8,128)(2,1)} %copy-done.38), kind=kOutput, calls=%fused_computation.7 | convolution fusion | flops 3764649984 | bytes 19660800 | tf_op jit(solution)/shard_map/dot_general | solution.py:19
  583.9 6.8 collective-permute-done.14
  592.1 13.6 %collective-permute-done.13 = bf16[128,1024]{1,0:T(8,128)(2,1)S(1)} collective-permute-done((bf16[128,1024]{1,0:T(8,128)(2,1)S(1)}, bf16[128,1024]{1,0:T(8,128)(2,1)S(1)}, u32[]{:S(2)}, u32[]{:S(2)}) %collective-permute-start.13) | collective-permute-done | bytes 262176 | tf_op jit(solution)/shard_map/ppermute | solution.py:32
  615.3 10.8 %fusion.20 = f32[256,2048]{1,0:T(8,128)} fusion(bf16[2048,3584]{1,0:T(8,128)(2,1)} %param.8, bf16[128,3584]{1,0:T(8,128)(2,1)} %collective-permute-done.25, bf16[64,3584]{1,0:T(8,128)(2,1)S(1)} %get-tuple-element.12, bf16[64,3584]{1,0:T(8,128)(2,1)S(1)} %get-tuple-element.14), kind=kOutput, calls=%fused_computation.43 | convolution fusion | flops 3763601408 | bytes 18612224 | tf_op jit(solution)/shard_map/dot_general | solution.py:19
  626.1 10.2 %fusion.1 = bf16[256,2048]{1,0:T(8,128)(2,1)S(1)} fusion(f32[256,2048]{1,0:T(8,128)} %fusion.20, bf16[2048,3584]{1,0:T(8,128)(2,1)} %param.7, bf16[128,3584]{1,0:T(8,128)(2,1)} %collective-permute-done.23, bf16[64,3584]{1,0:T(8,128)(2,1)} %copy-done.33, bf16[64,3584]{1,0:T(8,128)(2,1)S(1)} %copy-done.32), kind=kOutput, calls=%fused_computation.8 | convolution fusion | flops 3764649984 | bytes 19660800 | tf_op jit(solution)/shard_map/dot_general | solution.py:19
  645.9 5.6 collective-permute-done.29
  651.6 15.7 %collective-permute-done.28 = bf16[128,1024]{1,0:T(8,128)(2,1)S(1)} collective-permute-done((bf16[128,1024]{1,0:T(8,128)(2,1)S(1)}, bf16[128,1024]{1,0:T(8,128)(2,1)S(1)}, u32[]{:S(2)}, u32[]{:S(2)}) %collective-permute-start.28) | collective-permute-done | bytes 262176 | tf_op jit(solution)/shard_map/ppermute | solution.py:32
  674.9 10.8 %fusion.31 = f32[256,2048]{1,0:T(8,128)} fusion(bf16[2048,3584]{1,0:T(8,128)(2,1)} %param.8, bf16[128,3584]{1,0:T(8,128)(2,1)} %collective-permute-done.40, bf16[64,3584]{1,0:T(8,128)(2,1)S(1)} %copy-done.30, bf16[64,3584]{1,0:T(8,128)(2,1)S(1)} %get-tuple-element.10), kind=kOutput, calls=%fused_computation.54 | convolution fusion | flops 3763601408 | bytes 18612224 | tf_op jit(solution)/shard_map/dot_general | solution.py:19
  685.6 11.0 %fusion.2 = bf16[256,2048]{1,0:T(8,128)(2,1)} fusion(f32[256,2048]{1,0:T(8,128)} %fusion.31, bf16[2048,3584]{1,0:T(8,128)(2,1)} %param.7, bf16[128,3584]{1,0:T(8,128)(2,1)} %collective-permute-done.38, bf16[64,3584]{1,0:T(8,128)(2,1)S(1)} %copy-done.35, bf16[64,3584]{1,0:T(8,128)(2,1)S(1)} %get-tuple-element.26), kind=kOutput, calls=%fused_computation.9 | convolution fusion | flops 3764649984 | bytes 19660800 | tf_op jit(solution)/shard_map/dot_general | solution.py:19
  707.7 5.5 collective-permute-done.44
  713.2 15.3 %collective-permute-done.43 = bf16[128,1024]{1,0:T(8,128)(2,1)S(1)} collective-permute-done((bf16[128,1024]{1,0:T(8,128)(2,1)S(1)}, bf16[128,1024]{1,0:T(8,128)(2,1)S(1)}, u32[]{:S(2)}, u32[]{:S(2)}) %collective-permute-start.43) | collective-permute-done | bytes 262176 | tf_op jit(solution)/shard_map/ppermute | solution.py:32
  729.5 10.8 %fusion.42 = f32[256,2048]{1,0:T(8,128)} fusion(bf16[2048,3584]{1,0:T(8,128)(2,1)} %param.8, bf16[128,3584]{1,0:T(8,128)(2,1)} %collective-permute-done.55, bf16[64,3584]{1,0:T(8,128)(2,1)S(1)} %get-tuple-element.4, bf16[64,3584]{1,0:T(8,128)(2,1)S(1)} %get-tuple-element.6), kind=kOutput, calls=%fused_computation.65 | convolution fusion | flops 3763601408 | bytes 18612224 | tf_op jit(solution)/shard_map/dot_general | solution.py:19
  740.2 11.4 %fusion.3 = bf16[256,2048]{1,0:T(8,128)(2,1)} fusion(f32[256,2048]{1,0:T(8,128)} %fusion.42, bf16[2048,3584]{1,0:T(8,128)(2,1)} %param.7, bf16[128,3584]{1,0:T(8,128)(2,1)} %collective-permute-done.53, bf16[64,3584]{1,0:T(8,128)(2,1)} %copy-done.37, bf16[64,3584]{1,0:T(8,128)(2,1)} %copy-done.36), kind=kOutput, calls=%fused_computation.10 | convolution fusion | flops 3764649984 | bytes 19660800 | tf_op jit(solution)/shard_map/dot_general | solution.py:19
  755.0 21.2 %multiply_convert_fusion.1 = bf16[2048,3584]{1,0:T(8,128)(2,1)} fusion(bf16[1024,3584]{1,0:T(8,128)(2,1)} %constant_dynamic-update-slice_fusion, bf16[256,2048]{0,1:T(8,128)(2,1)} %bitcast.84, bf16[256,2048]{0,1:T(8,128)(2,1)S(1)} %bitcast.80, bf16[256,2048]{0,1:T(8,128)(2,1)S(1)} %bitcast.76, bf16[256,2048]{0,1:T(8,128)(2,1)S(1)} %bitcast.72), kind=kOutput, calls=%fused_computation.1 | convolution fusion | flops 15063842816 | bytes 26214400 | tf_op jit(solution)/shard_map/dot_general | solution.py:25
  785.7 20.8 %multiply_convert_fusion = bf16[2048,3584]{1,0:T(8,128)(2,1)} fusion(bf16[1024,3584]{1,0:T(8,128)(2,1)} %constant_dynamic-update-slice_fusion.12, bf16[256,2048]{0,1:T(8,128)(2,1)S(1)} %bitcast.85, bf16[256,2048]{0,1:T(8,128)(2,1)S(1)} %bitcast.81, bf16[256,2048]{0,1:T(8,128)(2,1)S(1)} %bitcast.77, bf16[256,2048]{0,1:T(8,128)(2,1)S(1)} %bitcast.73), kind=kOutput, calls=%fused_computation | convolution fusion | flops 15063842816 | bytes 26214400 | tf_op jit(solution)/shard_map/dot_general | solution.py:25
  (318 shorter events, 182.2 us)
Async XLA Ops:
  7.2 51.6 %all-gather.9.cloned.1.call-start = ((), (), s32[]{:S(2)}) async-start(), calls=%async_computation | async-start | bytes 2621440 | tf_op jit(solution)/shard_map/all_gather | solution.py:82
  9.8 95.8 %all-gather.11.cloned.1.call-start = ((), (), s32[]{:S(2)}) async-start(), calls=%async_computation.1 | async-start | bytes 2621440 | tf_op jit(solution)/shard_map/all_gather | solution.py:82
  10.8 141.7 %all-gather.13.cloned.1.call-start = ((), (), s32[]{:S(2)}) async-start(), calls=%async_computation.2 | async-start | bytes 2621440 | tf_op jit(solution)/shard_map/all_gather | solution.py:82
  11.7 186.9 %all-gather.15.cloned.1.call-start = ((), (), s32[]{:S(2)}) async-start(), calls=%async_computation.3 | async-start | bytes 2621440 | tf_op jit(solution)/shard_map/all_gather | solution.py:82
  61.6 139.8 %collective-permute-start = (bf16[2,2,128,1024]{3,2,1,0:T(8,128)(2,1)}, bf16[2,2,128,1024]{3,2,1,0:T(8,128)(2,1)}, u32[]{:S(2)}, u32[]{:S(2)}) collective-permute-start(bf16[2,2,128,1024]{3,2,1,0:T(8,128)(2,1)} %get-tuple-element.58), channel_id=1, source_target_pairs={{0,2},{2,0},{1,3},{3,1},{4,6},{6,4},{5,7},{7,5},{8,10},{10,8},{9,1... | collective-permute-start | bytes 3145736 | tf_op jit(solution)/shard_map/ppermute | solution.py:32
  108.7 116.2 %collective-permute-start.15 = (bf16[2,2,128,1024]{3,2,1,0:T(8,128)(2,1)}, bf16[2,2,128,1024]{3,2,1,0:T(8,128)(2,1)}, u32[]{:S(2)}, u32[]{:S(2)}) collective-permute-start(bf16[2,2,128,1024]{3,2,1,0:T(8,128)(2,1)} %get-tuple-element.54), channel_id=1, source_target_pairs={{0,2},{2,0},{1,3},{3,1},{4,6},{6,4},{5,7},{7,5},{8,10},{10,8},{9,1... | collective-permute-start | bytes 3145736 | tf_op jit(solution)/shard_map/ppermute | solution.py:32
  155.3 92.7 %collective-permute-start.30 = (bf16[2,2,128,1024]{3,2,1,0:T(8,128)(2,1)}, bf16[2,2,128,1024]{3,2,1,0:T(8,128)(2,1)}, u32[]{:S(2)}, u32[]{:S(2)}) collective-permute-start(bf16[2,2,128,1024]{3,2,1,0:T(8,128)(2,1)} %get-tuple-element.50), channel_id=1, source_target_pairs={{0,2},{2,0},{1,3},{3,1},{4,6},{6,4},{5,7},{7,5},{8,10},{10,8},{9,1... | collective-permute-start | bytes 3145736 | tf_op jit(solution)/shard_map/ppermute | solution.py:32
  201.4 79.4 %collective-permute-start.45 = (bf16[2,2,128,1024]{3,2,1,0:T(8,128)(2,1)}, bf16[2,2,128,1024]{3,2,1,0:T(8,128)(2,1)}, u32[]{:S(2)}, u32[]{:S(2)}) collective-permute-start(bf16[2,2,128,1024]{3,2,1,0:T(8,128)(2,1)} %get-tuple-element.46), channel_id=1, source_target_pairs={{0,2},{2,0},{1,3},{3,1},{4,6},{6,4},{5,7},{7,5},{8,10},{10,8},{9,1... | collective-permute-start | bytes 3145736 | tf_op jit(solution)/shard_map/ppermute | solution.py:32
  305.0 60.8 %collective-permute-start.3 = (f32[128,3584]{1,0:T(8,128)}, f32[128,3584]{1,0:T(8,128)}, u32[]{:S(2)}, u32[]{:S(2)}) collective-permute-start(f32[128,3584]{1,0:T(8,128)} %slice.205), channel_id=1, source_target_pairs={{0,2},{2,0},{1,3},{3,1},{4,6},{6,4},{5,7},{7,5},{8,10},{10,8},{9,1... | collective-permute-start | bytes 5505032 | tf_op jit(solution)/shard_map/ppermute | solution.py:32
  315.8 52.2 %collective-permute-start.1 = (f32[128,3584]{1,0:T(8,128)}, f32[128,3584]{1,0:T(8,128)}, u32[]{:S(2)}, u32[]{:S(2)}) collective-permute-start(f32[128,3584]{1,0:T(8,128)} %slice.202), channel_id=1, source_target_pairs={{0,2},{2,0},{1,3},{3,1},{4,6},{6,4},{5,7},{7,5},{8,10},{10,8},{9,1... | collective-permute-start | bytes 5505032 | tf_op jit(solution)/shard_map/ppermute | solution.py:32
  319.8 51.3 %collective-permute-start.5 = (f32[128,3584]{1,0:T(8,128)}, f32[128,3584]{1,0:T(8,128)}, u32[]{:S(2)}, u32[]{:S(2)}) collective-permute-start(f32[128,3584]{1,0:T(8,128)} %slice.207), channel_id=1, source_target_pairs={{0,2},{2,0},{1,3},{3,1},{4,6},{6,4},{5,7},{7,5},{8,10},{10,8},{9,1... | collective-permute-start | bytes 5505032 | tf_op jit(solution)/shard_map/ppermute | solution.py:32
  321.5 52.6 %collective-permute-start.18 = (f32[128,3584]{1,0:T(8,128)}, f32[128,3584]{1,0:T(8,128)}, u32[]{:S(2)}, u32[]{:S(2)}) collective-permute-start(f32[128,3584]{1,0:T(8,128)} %slice.215), channel_id=1, source_target_pairs={{0,2},{2,0},{1,3},{3,1},{4,6},{6,4},{5,7},{7,5},{8,10},{10,8},{9,1... | collective-permute-start | bytes 5505032 | tf_op jit(solution)/shard_map/ppermute | solution.py:32
  334.0 42.4 %collective-permute-start.16 = (f32[128,3584]{1,0:T(8,128)}, f32[128,3584]{1,0:T(8,128)}, u32[]{:S(2)}, u32[]{:S(2)}) collective-permute-start(f32[128,3584]{1,0:T(8,128)} %slice.212), channel_id=1, source_target_pairs={{0,2},{2,0},{1,3},{3,1},{4,6},{6,4},{5,7},{7,5},{8,10},{10,8},{9,1... | collective-permute-start | bytes 5505032 | tf_op jit(solution)/shard_map/ppermute | solution.py:32
  386.8 19.9 %collective-permute-start.2 = (bf16[64,3584]{1,0:T(8,128)(2,1)S(1)}, bf16[64,3584]{1,0:T(8,128)(2,1)S(1)}, u32[]{:S(2)}, u32[]{:S(2)}) collective-permute-start(bf16[64,3584]{1,0:T(8,128)(2,1)S(1)} %copy-done.46), channel_id=1, source_target_pairs={{0,1},{1,0},{2,3},{3,2},{4,5},{5,4},{6,7},{7,6},{8,9},{9,8},{10,11... | collective-permute-start | bytes 1376264 | tf_op jit(solution)/shard_map/ppermute | solution.py:32
  389.3 27.3 %collective-permute-start.6 = (bf16[64,3584]{1,0:T(8,128)(2,1)S(1)}, bf16[64,3584]{1,0:T(8,128)(2,1)S(1)}, u32[]{:S(2)}, u32[]{:S(2)}) collective-permute-start(bf16[64,3584]{1,0:T(8,128)(2,1)S(1)} %copy-done.48), channel_id=1, source_target_pairs={{0,1},{1,0},{2,3},{3,2},{4,5},{5,4},{6,7},{7,6},{8,9},{9,8},{10,11... | collective-permute-start | bytes 1376264 | tf_op jit(solution)/shard_map/ppermute | solution.py:32
  392.6 33.7 %collective-permute-start.19 = (bf16[64,3584]{1,0:T(8,128)(2,1)S(1)}, bf16[64,3584]{1,0:T(8,128)(2,1)S(1)}, u32[]{:S(2)}, u32[]{:S(2)}) collective-permute-start(bf16[64,3584]{1,0:T(8,128)(2,1)S(1)} %dynamic-slice_convert_fusion.7), channel_id=1, source_target_pairs={{0,1},{1,0},{2,3},{3,2},{4,5},{5,4},{6,7},{7,6},{8,9},{9,8},{10,11... | collective-permute-start | bytes 1376264 | tf_op jit(solution)/shard_map/ppermute | solution.py:32
  393.6 42.6 %collective-permute-start.17 = (bf16[64,3584]{1,0:T(8,128)(2,1)S(1)}, bf16[64,3584]{1,0:T(8,128)(2,1)S(1)}, u32[]{:S(2)}, u32[]{:S(2)}) collective-permute-start(bf16[64,3584]{1,0:T(8,128)(2,1)S(1)} %copy-done.47), channel_id=1, source_target_pairs={{0,1},{1,0},{2,3},{3,2},{4,5},{5,4},{6,7},{7,6},{8,9},{9,8},{10,11... | collective-permute-start | bytes 1376264 | tf_op jit(solution)/shard_map/ppermute | solution.py:32
  396.9 49.2 %collective-permute-start.21 = (bf16[64,3584]{1,0:T(8,128)(2,1)S(1)}, bf16[64,3584]{1,0:T(8,128)(2,1)S(1)}, u32[]{:S(2)}, u32[]{:S(2)}) collective-permute-start(bf16[64,3584]{1,0:T(8,128)(2,1)S(1)} %dynamic-slice_convert_fusion.6), channel_id=1, source_target_pairs={{0,1},{1,0},{2,3},{3,2},{4,5},{5,4},{6,7},{7,6},{8,9},{9,8},{10,11... | collective-permute-start | bytes 1376264 | tf_op jit(solution)/shard_map/ppermute | solution.py:32
  406.7 49.2 %collective-permute-start.34 = (bf16[64,3584]{1,0:T(8,128)(2,1)S(1)}, bf16[64,3584]{1,0:T(8,128)(2,1)S(1)}, u32[]{:S(2)}, u32[]{:S(2)}) collective-permute-start(bf16[64,3584]{1,0:T(8,128)(2,1)S(1)} %dynamic-slice_convert_fusion.4), channel_id=1, source_target_pairs={{0,1},{1,0},{2,3},{3,2},{4,5},{5,4},{6,7},{7,6},{8,9},{9,8},{10,11... | collective-permute-start | bytes 1376264 | tf_op jit(solution)/shard_map/ppermute | solution.py:32
  416.6 49.2 %collective-permute-start.32 = (bf16[64,3584]{1,0:T(8,128)(2,1)S(1)}, bf16[64,3584]{1,0:T(8,128)(2,1)S(1)}, u32[]{:S(2)}, u32[]{:S(2)}) collective-permute-start(bf16[64,3584]{1,0:T(8,128)(2,1)S(1)} %dynamic-slice_convert_fusion.5), channel_id=1, source_target_pairs={{0,1},{1,0},{2,3},{3,2},{4,5},{5,4},{6,7},{7,6},{8,9},{9,8},{10,11... | collective-permute-start | bytes 1376264 | tf_op jit(solution)/shard_map/ppermute | solution.py:32
  426.4 49.2 %collective-permute-start.36 = (bf16[64,3584]{1,0:T(8,128)(2,1)S(1)}, bf16[64,3584]{1,0:T(8,128)(2,1)S(1)}, u32[]{:S(2)}, u32[]{:S(2)}) collective-permute-start(bf16[64,3584]{1,0:T(8,128)(2,1)S(1)} %dynamic-slice_convert_fusion.3), channel_id=1, source_target_pairs={{0,1},{1,0},{2,3},{3,2},{4,5},{5,4},{6,7},{7,6},{8,9},{9,8},{10,11... | collective-permute-start | bytes 1376264 | tf_op jit(solution)/shard_map/ppermute | solution.py:32
  436.2 49.2 %collective-permute-start.49 = (bf16[64,3584]{1,0:T(8,128)(2,1)S(1)}, bf16[64,3584]{1,0:T(8,128)(2,1)S(1)}, u32[]{:S(2)}, u32[]{:S(2)}) collective-permute-start(bf16[64,3584]{1,0:T(8,128)(2,1)S(1)} %dynamic-slice_convert_fusion.1), channel_id=1, source_target_pairs={{0,1},{1,0},{2,3},{3,2},{4,5},{5,4},{6,7},{7,6},{8,9},{9,8},{10,11... | collective-permute-start | bytes 1376264 | tf_op jit(solution)/shard_map/ppermute | solution.py:32
  446.0 49.2 %collective-permute-start.47 = (bf16[64,3584]{1,0:T(8,128)(2,1)S(1)}, bf16[64,3584]{1,0:T(8,128)(2,1)S(1)}, u32[]{:S(2)}, u32[]{:S(2)}) collective-permute-start(bf16[64,3584]{1,0:T(8,128)(2,1)S(1)} %dynamic-slice_convert_fusion.2), channel_id=1, source_target_pairs={{0,1},{1,0},{2,3},{3,2},{4,5},{5,4},{6,7},{7,6},{8,9},{9,8},{10,11... | collective-permute-start | bytes 1376264 | tf_op jit(solution)/shard_map/ppermute | solution.py:32
  455.9 49.2 %collective-permute-start.51 = (bf16[64,3584]{1,0:T(8,128)(2,1)S(1)}, bf16[64,3584]{1,0:T(8,128)(2,1)S(1)}, u32[]{:S(2)}, u32[]{:S(2)}) collective-permute-start(bf16[64,3584]{1,0:T(8,128)(2,1)S(1)} %dynamic-slice_convert_fusion), channel_id=1, source_target_pairs={{0,1},{1,0},{2,3},{3,2},{4,5},{5,4},{6,7},{7,6},{8,9},{9,8},{10,11... | collective-permute-start | bytes 1376264 | tf_op jit(solution)/shard_map/ppermute | solution.py:32
  465.7 49.2 %collective-permute-start.9 = (bf16[64,3584]{1,0:T(8,128)(2,1)S(1)}, bf16[64,3584]{1,0:T(8,128)(2,1)S(1)}, u32[]{:S(2)}, u32[]{:S(2)}) collective-permute-start(bf16[64,3584]{1,0:T(8,128)(2,1)S(1)} %get-tuple-element.42), channel_id=1, source_target_pairs={{0,1},{1,0},{2,3},{3,2},{4,5},{5,4},{6,7},{7,6},{8,9},{9,8},{10,11... | collective-permute-start | bytes 1376264 | tf_op jit(solution)/shard_map/ppermute | solution.py:32
  475.5 72.8 %collective-permute-start.24 = (bf16[64,3584]{1,0:T(8,128)(2,1)S(1)}, bf16[64,3584]{1,0:T(8,128)(2,1)S(1)}, u32[]{:S(2)}, u32[]{:S(2)}) collective-permute-start(bf16[64,3584]{1,0:T(8,128)(2,1)S(1)} %get-tuple-element.40), channel_id=1, source_target_pairs={{0,1},{1,0},{2,3},{3,2},{4,5},{5,4},{6,7},{7,6},{8,9},{9,8},{10,11... | collective-permute-start | bytes 1376264 | tf_op jit(solution)/shard_map/ppermute | solution.py:32
  485.4 124.8 %collective-permute-start.39 = (bf16[64,3584]{1,0:T(8,128)(2,1)S(1)}, bf16[64,3584]{1,0:T(8,128)(2,1)}, u32[]{:S(2)}, u32[]{:S(2)}) collective-permute-start(bf16[64,3584]{1,0:T(8,128)(2,1)S(1)} %get-tuple-element.38), channel_id=1, source_target_pairs={{0,1},{1,0},{2,3},{3,2},{4,5},{5,4},{6,7},{7,6},{8,9},{9,8},{10,11... | collective-permute-start | bytes 1376264 | tf_op jit(solution)/shard_map/ppermute | solution.py:32
  495.2 49.2 %collective-permute-start.7 = (bf16[64,3584]{1,0:T(8,128)(2,1)S(1)}, bf16[64,3584]{1,0:T(8,128)(2,1)S(1)}, u32[]{:S(2)}, u32[]{:S(2)}) collective-permute-start(bf16[64,3584]{1,0:T(8,128)(2,1)S(1)} %get-tuple-element.41), channel_id=1, source_target_pairs={{0,1},{1,0},{2,3},{3,2},{4,5},{5,4},{6,7},{7,6},{8,9},{9,8},{10,11... | collective-permute-start | bytes 1376264 | tf_op jit(solution)/shard_map/ppermute | solution.py:32
  505.0 72.2 %collective-permute-start.22 = (bf16[64,3584]{1,0:T(8,128)(2,1)S(1)}, bf16[64,3584]{1,0:T(8,128)(2,1)}, u32[]{:S(2)}, u32[]{:S(2)}) collective-permute-start(bf16[64,3584]{1,0:T(8,128)(2,1)S(1)} %get-tuple-element.39), channel_id=1, source_target_pairs={{0,1},{1,0},{2,3},{3,2},{4,5},{5,4},{6,7},{7,6},{8,9},{9,8},{10,11... | collective-permute-start | bytes 1376264 | tf_op jit(solution)/shard_map/ppermute | solution.py:32
  516.7 30.5 %collective-permute-start.10 = (bf16[128,3584]{1,0:T(8,128)(2,1)S(1)}, bf16[128,3584]{1,0:T(8,128)(2,1)S(1)}, u32[]{:S(2)}, u32[]{:S(2)}) collective-permute-start(bf16[128,3584]{1,0:T(8,128)(2,1)S(1)} %pad_maximum_fusion.3), channel_id=1, source_target_pairs={{0,2},{2,0},{1,3},{3,1},{4,6},{6,4},{5,7},{7,5},{8,10},{10,8},{9,1... | collective-permute-start | bytes 2752520 | tf_op jit(solution)/shard_map/ppermute | solution.py:32
  551.1 56.9 %collective-permute-start.25 = (bf16[128,3584]{1,0:T(8,128)(2,1)}, bf16[128,3584]{1,0:T(8,128)(2,1)}, u32[]{:S(2)}, u32[]{:S(2)}) collective-permute-start(bf16[128,3584]{1,0:T(8,128)(2,1)} %pad_maximum_fusion.5), channel_id=1, source_target_pairs={{0,2},{2,0},{1,3},{3,1},{4,6},{6,4},{5,7},{7,5},{8,10},{10,8},{9,1... | collective-permute-start | bytes 2752520 | tf_op jit(solution)/shard_map/ppermute | solution.py:32
  581.9 23.7 %collective-permute-start.13 = (bf16[128,1024]{1,0:T(8,128)(2,1)S(1)}, bf16[128,1024]{1,0:T(8,128)(2,1)S(1)}, u32[]{:S(2)}, u32[]{:S(2)}) collective-permute-start(bf16[128,1024]{1,0:T(8,128)(2,1)S(1)} %get-tuple-element.68), channel_id=1, source_target_pairs={{0,8},{4,12},{8,0},{12,4},{1,9},{5,13},{9,1},{13,5},{2,10},{6,14},... | collective-permute-start | bytes 786440 | tf_op jit(solution)/shard_map/ppermute | solution.py:32
  582.1 24.9 %collective-permute-start.12 = (bf16[128,1024]{1,0:T(8,128)(2,1)S(1)}, bf16[128,1024]{1,0:T(8,128)(2,1)S(1)}, u32[]{:S(2)}, u32[]{:S(2)}) collective-permute-start(bf16[128,1024]{1,0:T(8,128)(2,1)S(1)} %get-tuple-element.67), channel_id=1, source_target_pairs={{0,4},{4,8},{8,12},{12,0},{1,5},{5,9},{9,13},{13,1},{2,6},{6,10},{... | collective-permute-start | bytes 786440 | tf_op jit(solution)/shard_map/ppermute | solution.py:32
  590.8 79.7 %collective-permute-start.54 = (bf16[64,3584]{1,0:T(8,128)(2,1)S(1)}, bf16[64,3584]{1,0:T(8,128)(2,1)}, u32[]{:S(2)}, u32[]{:S(2)}) collective-permute-start(bf16[64,3584]{1,0:T(8,128)(2,1)S(1)} %get-tuple-element.36), channel_id=1, source_target_pairs={{0,1},{1,0},{2,3},{3,2},{4,5},{5,4},{6,7},{7,6},{8,9},{9,8},{10,11... | collective-permute-start | bytes 1376264 | tf_op jit(solution)/shard_map/ppermute | solution.py:32
  605.7 33.2 %collective-permute-start.37 = (bf16[64,3584]{1,0:T(8,128)(2,1)S(1)}, bf16[64,3584]{1,0:T(8,128)(2,1)}, u32[]{:S(2)}, u32[]{:S(2)}) collective-permute-start(bf16[64,3584]{1,0:T(8,128)(2,1)S(1)} %get-tuple-element.37), channel_id=1, source_target_pairs={{0,1},{1,0},{2,3},{3,2},{4,5},{5,4},{6,7},{7,6},{8,9},{9,8},{10,11... | collective-permute-start | bytes 1376264 | tf_op jit(solution)/shard_map/ppermute | solution.py:32
  607.0 19.1 %collective-permute-start.23 = (bf16[128,3584]{1,0:T(8,128)(2,1)S(1)}, bf16[128,3584]{1,0:T(8,128)(2,1)}, u32[]{:S(2)}, u32[]{:S(2)}) collective-permute-start(bf16[128,3584]{1,0:T(8,128)(2,1)S(1)} %pad_maximum_fusion.4), channel_id=1, source_target_pairs={{0,2},{2,0},{1,3},{3,1},{4,6},{6,4},{5,7},{7,5},{8,10},{10,8},{9,1... | collective-permute-start | bytes 2752520 | tf_op jit(solution)/shard_map/ppermute | solution.py:32
  614.8 53.4 %collective-permute-start.40 = (bf16[128,3584]{1,0:T(8,128)(2,1)}, bf16[128,3584]{1,0:T(8,128)(2,1)}, u32[]{:S(2)}, u32[]{:S(2)}) collective-permute-start(bf16[128,3584]{1,0:T(8,128)(2,1)} %pad_maximum_fusion.7), channel_id=1, source_target_pairs={{0,2},{2,0},{1,3},{3,1},{4,6},{6,4},{5,7},{7,5},{8,10},{10,8},{9,1... | collective-permute-start | bytes 2752520 | tf_op jit(solution)/shard_map/ppermute | solution.py:32
  642.3 25.0 %collective-permute-start.28 = (bf16[128,1024]{1,0:T(8,128)(2,1)S(1)}, bf16[128,1024]{1,0:T(8,128)(2,1)S(1)}, u32[]{:S(2)}, u32[]{:S(2)}) collective-permute-start(bf16[128,1024]{1,0:T(8,128)(2,1)S(1)} %get-tuple-element.71), channel_id=1, source_target_pairs={{0,8},{4,12},{8,0},{12,4},{1,9},{5,13},{9,1},{13,5},{2,10},{6,14},... | collective-permute-start | bytes 786440 | tf_op jit(solution)/shard_map/ppermute | solution.py:32
  643.7 23.5 %collective-permute-start.27 = (bf16[128,1024]{1,0:T(8,128)(2,1)S(1)}, bf16[128,1024]{1,0:T(8,128)(2,1)S(1)}, u32[]{:S(2)}, u32[]{:S(2)}) collective-permute-start(bf16[128,1024]{1,0:T(8,128)(2,1)S(1)} %get-tuple-element.70), channel_id=1, source_target_pairs={{0,4},{4,8},{8,12},{12,0},{1,5},{5,9},{9,13},{13,1},{2,6},{6,10},{... | collective-permute-start | bytes 786440 | tf_op jit(solution)/shard_map/ppermute | solution.py:32
  651.6 48.5 %collective-permute-start.52 = (bf16[64,3584]{1,0:T(8,128)(2,1)S(1)}, bf16[64,3584]{1,0:T(8,128)(2,1)}, u32[]{:S(2)}, u32[]{:S(2)}) collective-permute-start(bf16[64,3584]{1,0:T(8,128)(2,1)S(1)} %get-tuple-element.35), channel_id=1, source_target_pairs={{0,1},{1,0},{2,3},{3,2},{4,5},{5,4},{6,7},{7,6},{8,9},{9,8},{10,11... | collective-permute-start | bytes 1376264 | tf_op jit(solution)/shard_map/ppermute | solution.py:32
  674.4 55.1 %collective-permute-start.55 = (bf16[128,3584]{1,0:T(8,128)(2,1)}, bf16[128,3584]{1,0:T(8,128)(2,1)}, u32[]{:S(2)}, u32[]{:S(2)}) collective-permute-start(bf16[128,3584]{1,0:T(8,128)(2,1)} %pad_maximum_fusion.9), channel_id=1, source_target_pairs={{0,2},{2,0},{1,3},{3,1},{4,6},{6,4},{5,7},{7,5},{8,10},{10,8},{9,1... | collective-permute-start | bytes 2752520 | tf_op jit(solution)/shard_map/ppermute | solution.py:32
  703.6 24.9 %collective-permute-start.43 = (bf16[128,1024]{1,0:T(8,128)(2,1)S(1)}, bf16[128,1024]{1,0:T(8,128)(2,1)S(1)}, u32[]{:S(2)}, u32[]{:S(2)}) collective-permute-start(bf16[128,1024]{1,0:T(8,128)(2,1)S(1)} %get-tuple-element.74), channel_id=1, source_target_pairs={{0,8},{4,12},{8,0},{12,4},{1,9},{5,13},{9,1},{13,5},{2,10},{6,14},... | collective-permute-start | bytes 786440 | tf_op jit(solution)/shard_map/ppermute | solution.py:32
  705.2 23.3 %collective-permute-start.42 = (bf16[128,1024]{1,0:T(8,128)(2,1)S(1)}, bf16[128,1024]{1,0:T(8,128)(2,1)S(1)}, u32[]{:S(2)}, u32[]{:S(2)}) collective-permute-start(bf16[128,1024]{1,0:T(8,128)(2,1)S(1)} %get-tuple-element.73), channel_id=1, source_target_pairs={{0,4},{4,8},{8,12},{12,0},{1,5},{5,9},{9,13},{13,1},{2,6},{6,10},{... | collective-permute-start | bytes 786440 | tf_op jit(solution)/shard_map/ppermute | solution.py:32
  707.6 32.6 %collective-permute-start.53 = (bf16[128,3584]{1,0:T(8,128)(2,1)S(1)}, bf16[128,3584]{1,0:T(8,128)(2,1)}, u32[]{:S(2)}, u32[]{:S(2)}) collective-permute-start(bf16[128,3584]{1,0:T(8,128)(2,1)S(1)} %pad_maximum_fusion.8), channel_id=1, source_target_pairs={{0,2},{2,0},{1,3},{3,1},{4,6},{6,4},{5,7},{7,5},{8,10},{10,8},{9,1... | collective-permute-start | bytes 2752520 | tf_op jit(solution)/shard_map/ppermute | solution.py:32
  752.7 25.7 %collective-permute-start.56 = (bf16[128,2048]{1,0:T(8,128)(2,1)S(1)}, bf16[128,2048]{1,0:T(8,128)(2,1)}, u32[]{:S(2)}, u32[]{:S(2)}) collective-permute-start(bf16[128,2048]{1,0:T(8,128)(2,1)S(1)} %slice.239), channel_id=1, source_target_pairs={{0,2},{2,0},{1,3},{3,1},{4,6},{6,4},{5,7},{7,5},{8,10},{10,8},{9,1... | collective-permute-start | bytes 1572872 | tf_op jit(solution)/shard_map/ppermute | solution.py:32
  781.8 24.7 %collective-permute-start.59 = (bf16[128,1024]{1,0:T(8,128)(2,1)}, bf16[128,1024]{1,0:T(8,128)(2,1)}, u32[]{:S(2)}, u32[]{:S(2)}) collective-permute-start(bf16[128,1024]{1,0:T(8,128)(2,1)} %get-tuple-element.78), channel_id=1, source_target_pairs={{0,12},{4,0},{8,4},{12,8},{1,13},{5,1},{9,5},{13,9},{2,14},{6,2},{... | collective-permute-start | bytes 786440 | tf_op jit(solution)/shard_map/ppermute | solution.py:32
  781.8 26.0 %collective-permute-start.58 = (bf16[128,1024]{1,0:T(8,128)(2,1)}, bf16[128,1024]{1,0:T(8,128)(2,1)}, u32[]{:S(2)}, u32[]{:S(2)}) collective-permute-start(bf16[128,1024]{1,0:T(8,128)(2,1)} %get-tuple-element.77), channel_id=1, source_target_pairs={{0,8},{4,12},{8,0},{12,4},{1,9},{5,13},{9,1},{13,5},{2,10},{6,14},... | collective-permute-start | bytes 786440 | tf_op jit(solution)/shard_map/ppermute | solution.py:32
  783.6 24.1 %collective-permute-start.57 = (bf16[128,1024]{1,0:T(8,128)(2,1)}, bf16[128,1024]{1,0:T(8,128)(2,1)}, u32[]{:S(2)}, u32[]{:S(2)}) collective-permute-start(bf16[128,1024]{1,0:T(8,128)(2,1)} %get-tuple-element.76), channel_id=1, source_target_pairs={{0,4},{4,8},{8,12},{12,0},{1,5},{5,9},{9,13},{13,1},{2,6},{6,10},{... | collective-permute-start | bytes 786440 | tf_op jit(solution)/shard_map/ppermute | solution.py:32
  (65 other events, 549.3 us)
Sparse Core Ops, SparseCore 0:
  10.1 48.6 all-gather.8
  61.0 44.6 all-gather.10
  107.8 44.6 all-gather.12
  153.9 44.6 all-gather.14

commit v2 on v1

v2 whole, which is shorter than its diff:
```python
import jax
import jax.numpy as jnp
from jax import lax
from jax.sharding import PartitionSpec as P

CHUNKS = 4


def swiglu_back(gate_sum, up_sum, back_sum):
    sigmoid_gate = jax.nn.sigmoid(gate_sum)
    grad_up = (back_sum * gate_sum * sigmoid_gate).astype(jnp.bfloat16)
    grad_gate = (back_sum * up_sum * sigmoid_gate * (1.0 + gate_sum * (1.0 - sigmoid_gate))).astype(
        jnp.bfloat16
    )
    return (grad_gate, grad_up)


def contract_last(left, right):
    return lax.dot_general(
        left, right, (((1,), (1,)), ((), ())), preferred_element_type=jnp.float32
    )


def contract_first(left, right):
    return lax.dot_general(
        left, right, (((0,), (0,)), ((), ())), preferred_element_type=jnp.float32
    )


def shift(block, axis, step):
    count = lax.axis_size(axis)
    return lax.ppermute(block, axis, [(i, (i + step) % count) for i in range(count)])


def block_of(array, index, size, dim=0):
    return lax.dynamic_slice_in_dim(array, index * size, size, dim)


def after(values, earlier):
    if not earlier:
        return values
    return lax.optimization_barrier((values, earlier))[0]


def scatter_parts(totals, axis):
    count, me = lax.axis_size(axis), lax.axis_index(axis)
    size = totals[0].shape[0] // count
    received = []
    for step in range(1, count):
        block = lax.rem(me + step, count)
        away = [block_of(total, block, size).astype(jnp.bfloat16) for total in totals]
        received.append(shift(jnp.stack(away), axis, step))
    return [block_of(total, me, size) for total in totals], received


def add_blocks(blocks):
    total = blocks[0].astype(jnp.float32)
    for block in blocks[1:]:
        total = total + block.astype(jnp.float32)
    return total.astype(jnp.bfloat16)


def send_rows(block, axis):
    return [shift(block, axis, step) for step in range(1, lax.axis_size(axis))]


def gather_rows(block, received, axis):
    count, me = lax.axis_size(axis), lax.axis_index(axis)
    size = block.shape[1]
    if count == 2:
        other = received[0]
        first = me == 0
        return jnp.concatenate(
            [jnp.where(first, block, other), jnp.where(first, other, block)], axis=1
        )
    whole = jnp.zeros((block.shape[0], count * size) + block.shape[2:], block.dtype)
    whole = lax.dynamic_update_slice_in_dim(whole, block, me * size, 1)
    for step, got in enumerate(received, 1):
        source = lax.rem(me + count - step, count)
        whole = lax.dynamic_update_slice_in_dim(whole, got, source * size, 1)
    return whole


def per_device(tokens, out_grad, gate_weight, up_weight, down_weight):
    rows, shard = tokens.shape
    weight_scale = float(rows * lax.axis_size("gy")) ** (-0.5)
    width = gate_weight.shape[0]
    shards = width // shard
    gy = lax.axis_index("gy")
    chunk = rows // CHUNKS

    def fetch(index):
        pair = jnp.stack(
            [
                tokens[index * chunk : (index + 1) * chunk],
                out_grad[index * chunk : (index + 1) * chunk],
            ]
        )
        return lax.all_gather(pair, "gx", axis=0)

    def load(blocks):
        mine = block_of(blocks, gy, shards)
        other = shift(block_of(blocks, 1 - gy, shards), "gy", 1)
        both = jnp.concatenate([mine, other], axis=2)
        both = both.transpose(1, 2, 0, 3).reshape(2, 2 * chunk, width)
        return both[0], both[1]

    def dots(features, grads, pending):
        parts = [
            jnp.dot(features, gate_weight, preferred_element_type=jnp.float32),
            jnp.dot(features, up_weight, preferred_element_type=jnp.float32),
        ]
        if pending is not None:
            spreads.append(spread(*after(pending, parts)))
            grads = after(grads, [spreads[-1][0]])
        parts.append(contract_last(grads, down_weight))
        away = shift(jnp.stack([part[chunk:] for part in parts]), "gy", 1)
        return [part[:chunk] for part in parts], away

    def send_sums(owns, others):
        return scatter_parts([own + others[i] for i, own in enumerate(owns)], "gz")

    def spread(pair, received):
        half = gather_rows(pair, received, "gz")
        return half, shift(half, "gy", 1)

    def input_part(grad_gate, grad_up):
        part = contract_last(grad_gate, gate_weight) + contract_last(grad_up, up_weight)
        part = part.astype(jnp.bfloat16)
        return part[:chunk], shift(part[chunk:], "gy", 1)

    def send_inputs(mine, other):
        first = gy == 0
        whole = jnp.concatenate(
            [jnp.where(first, mine, other), jnp.where(first, other, mine)], axis=1
        )
        count, me = lax.axis_size("gx"), lax.axis_index("gx")
        if count > 8:
            return [
                lax.psum_scatter(whole.astype(jnp.float32), "gx", scatter_dimension=1, tiled=True)
            ]
        blocks = [block_of(whole, me, shard, 1)]
        for step in range(1, count):
            away = block_of(whole, lax.rem(me + step, count), shard, 1)
            blocks.append(shift(away, "gx", step))
        return blocks

    blocks = [fetch(0)]
    loaded = [load(blocks[0])]
    summed, spreads, grads, in_parts, in_blocks, inputs = [], [], [], [], [], []
    last, pending = None, None
    for turn in range(CHUNKS + 2):
        if turn < CHUNKS:
            pairs = dots(*after(loaded[turn], last), pending)
            last = pairs[0]
            if turn + 1 < CHUNKS:
                blocks.append(fetch(turn + 1))
                loaded.append(load(after(blocks[turn + 1], last)))
        if turn >= 2:
            mine, other = after(spreads[turn - 2], last)
            grads.append([jnp.concatenate([mine[i], other[i]], axis=0) for i in range(2)])
            in_parts.append(input_part(*grads[-1]))
            last = [in_parts[-1][0]]
        if turn >= 3:
            in_blocks.append(send_inputs(*after(in_parts[turn - 3], last)))
        if turn >= 4:
            inputs.append(add_blocks(after(in_blocks[turn - 4], last)))
        if 1 <= turn <= CHUNKS:
            totals, received = after(summed[turn - 1], last)
            for got in received:
                totals = [total + got[i].astype(jnp.float32) for i, total in enumerate(totals)]
            small = swiglu_back(*totals)
            pending = (jnp.stack(small), send_rows(jnp.stack(small), "gz"))
            if turn + 1 >= CHUNKS:
                spreads.append(spread(*pending))
            last = list(small)
        if turn < CHUNKS:
            summed.append(send_sums(*after(pairs, last)))
            last = summed[-1][0]
    features = jnp.concatenate([pair[0] for pair in loaded], axis=0)
    gates = jnp.concatenate([pair[0] for pair in grads], axis=0)
    ups = jnp.concatenate([pair[1] for pair in grads], axis=0)
    gate_total = contract_first(features, after(gates, last))
    gate_grad = (gate_total * weight_scale).astype(jnp.bfloat16)
    in_blocks.append(send_inputs(*in_parts[-1]))
    inputs.append(add_blocks(after(in_blocks[-2], [gate_grad])))
    up_total = contract_first(features, after(ups, [gate_grad]))
    up_grad = (up_total * weight_scale).astype(jnp.bfloat16)
    inputs.append(add_blocks(after(in_blocks[-1], [up_grad])))
    return (jnp.concatenate(inputs, axis=0), gate_grad, up_grad)


def solution(mesh):
    return jax.shard_map(
        per_device,
        mesh=mesh,
        in_specs=(
            P(("judge", "gy"), ("gz", "gx")),
            P(("judge", "gy"), ("gz", "gx")),
            P(("gz", "gy"), "gx"),
            P(("gz", "gy"), "gx"),
            P("gx", ("gz", "gy")),
        ),
        out_specs=(
            P(("judge", "gy"), ("gz", "gx")),
            P(("judge", "gz", "gy"), "gx"),
            P(("judge", "gz", "gy"), "gx"),
        ),
        check_vma=False,
    )
```

time: 817 us -> 614 us (0.75); the launches traced: 818 us -> 606 us
  waiting for transfers between devices: 369 us -> 156 us
  local copies, waits for them, and re-layouts: 77.6 us -> 123 us
  matrix products: 247 us -> 204 us
  starting transfers between devices: 46.1 us -> 29.1 us
  other arithmetic: 64.2 us -> 78.5 us
    ppermute x60 -> x36, waiting for transfers between devices: 191 us -> 62.7 us  [shift(): lax.ppermute(block, axis, [(i, (i + step) % count) for i in range(count)])]
    all_gather x4, waiting for transfers between devices: 177 us -> 93.5 us  [fetch(): return lax.all_gather(pair, 'gx', axis=0)]
    dot_general x8, matrix products: 85 us -> 43.9 us  [the longest x4 27.6 us: dots(): jnp.dot(features, up_weight, preferred_element_type=jnp.float32)]
    another operation x1 -> x25, local copies, waits for them, and re-layouts: 1.76 us -> 35.6 us  [the longest x12 23.5 us: dots(): away = shift(jnp.stack([part[chunk:] for part in parts]), 'gy', 1)]
    unnamed x16 -> x6, other arithmetic: 19.6 us -> 0.01 us
    another operation x4 -> x16, other arithmetic: 3.38 us -> 21.9 us  [the longest x4 11.2 us: dots(): away = shift(jnp.stack([part[chunk:] for part in parts]), 'gy', 1)]
    ppermute x60 -> x36, starting transfers between devices: 45.9 us -> 28.7 us  [shift(): lax.ppermute(block, axis, [(i, (i + step) % count) for i in range(count)])]
    dynamic_slice x4 -> x16, local copies, waits for them, and re-layouts: 11.4 us -> 23.3 us  [block_of(): return lax.dynamic_slice_in_dim(array, index * size, size, dim)]
  transfers between devices with their start and end apart: 64 -> 40, of which waited for: 25 -> 10; matrix products, arithmetic and copies ran while one was open for 41% -> 60% of each run, Pallas kernels for 0% -> 0%
where the time goes in v2:
time: 614 us; the launch traced here: 606 us
  matrix products  204 us (33%)
  waiting for transfers between devices  156 us (25%)
  local copies, waits for them, and re-layouts  123 us (20%)
  other arithmetic  78.5 us (13%)
  starting transfers between devices  29.1 us (5%)
  between operations  15.3 us (2%)
    dot_general x12, matrix products, contract_last(): lax.dot_general(left, right, (((1,), (1,)), ((), ())), preferred_element_...  118 us
    all_gather x4, waiting for transfers between devices, fetch(): return lax.all_gather(pair, 'gx', axis=0)  93.5 us
    ppermute x36, waiting for transfers between devices, shift(): lax.ppermute(block, axis, [(i, (i + step) % count) for i in range(count)])  62.7 us
    dot_general x2, matrix products, contract_first(): lax.dot_general(left, right, (((0,), (0,)), ((), ())), preferred_element_...  41.6 us
    ppermute x36, starting transfers between devices, shift(): lax.ppermute(block, axis, [(i, (i + step) % count) for i in range(count)])  28.7 us
    dot_general x4, matrix products, dots(): jnp.dot(features, up_weight, preferred_element_type=jnp.float32)  27.6 us
    slice x12, local copies, waits for them, and re-layouts, load(): return (both[0], both[1])  25.2 us
    another operation x12, local copies, waits for them, and re-layouts, dots(): away = shift(jnp.stack([part[chunk:] for part in parts]), 'gy', 1)  23.5 us
  transfers between devices with their start and end apart: 40, of which 10 were waited for; matrix products, arithmetic and copies ran while one was open for 60% of the time, Pallas kernels for 0%

profile of v2, /device:TPU:0, one launch (start us, length us, event | category | flops | bytes accessed | tf_op | source)
XLA Modules:
  0.0 605.7 jit_solution(1893121176465537571)
XLA Ops:
  7.2 2.6 slice_bitcast_fusion.34
  10.8 48.7 %all-gather.9.cloned.1.call-done = bf16[8,128,1024]{2,1,0:T(8,128)(2,1)} async-done(((bf16[2,128,1024]{2,1,0:T(8,128)(2,1)}), bf16[8,128,1024]{2,1,0:T(8,128)(2,1)}) %all-gather.9.cloned.1.call-update) | async-done | bytes 2097168 | tf_op jit(solution)/shard_map/all_gather | solution.py:99
  61.3 2.6 collective-permute-done
  65.4 7.7 %fusion.95 = f32[256,3584]{1,0:T(8,128)S(1)} fusion(bf16[256,2048]{0,1:T(8,128)(2,1)S(1)} %bitcast.305, bf16[3584,2048]{1,0:T(8,128)(2,1)} %param.9), kind=kOutput, calls=%fused_computation.295 | convolution fusion | flops 3758096384 | bytes 19398656 | tf_op jit(solution)/shard_map/dot_general | solution.py:19
  73.5 7.5 %fusion.94 = f32[256,3584]{1,0:T(8,128)S(1)} fusion(bf16[256,2048]{0,1:T(8,128)(2,1)S(1)} %bitcast.270, bf16[2048,3584]{1,0:T(8,128)(2,1)} %param.8), kind=kOutput, calls=%fused_computation.294 | convolution fusion | flops 3758096384 | bytes 19398656 | tf_op jit(solution)/shard_map/dot_general | solution.py:111
  83.3 4.0 fusion.93
  88.8 2.8 pad_maximum_fusion
  92.7 44.8 %all-gather.11.cloned.1.call-done = bf16[8,128,1024]{2,1,0:T(8,128)(2,1)} async-done(((bf16[2,128,1024]{2,1,0:T(8,128)(2,1)}), bf16[8,128,1024]{2,1,0:T(8,128)(2,1)}) %all-gather.11.cloned.1.call-update) | async-done | bytes 2097168 | tf_op jit(solution)/shard_map/all_gather | solution.py:99
  137.5 2.8 constant_dynamic-slice_fusion.14
  149.6 4.7 bitcast_add_fusion.9
  157.8 8.2 %fusion.97 = f32[256,3584]{1,0:T(8,128)S(1)} fusion(bf16[256,2048]{0,1:T(8,128)(2,1)S(1)} %bitcast.274, bf16[2048,3584]{1,0:T(8,128)(2,1)} %param.8), kind=kOutput, calls=%fused_computation.297 | convolution fusion | flops 3758096384 | bytes 19398656 | tf_op jit(solution)/shard_map/dot_general | solution.py:111
  166.0 4.3 fusion.96
  170.3 11.4 %fusion.98 = f32[256,3584]{1,0:T(8,128)} fusion(bf16[256,2048]{0,1:T(8,128)(2,1)} %bitcast.304, bf16[3584,2048]{1,0:T(8,128)(2,1)} %param.9), kind=kOutput, calls=%fused_computation.298 | convolution fusion | flops 3758096384 | bytes 19398656 | tf_op jit(solution)/shard_map/dot_general | solution.py:19
  181.7 3.5 slice_bitcast_fusion.6
  188.2 2.8 pad_maximum_fusion.1
  205.6 12.6 %copy.20 = bf16[1,256,2,1024]{1,3,2,0:T(8,128)(2,1)S(1)} copy(bf16[1,256,2,1024]{3,1,0,2:T(8,128)(2,1)} %get-tuple-element.210) | data formatting | bytes 2097152 | tf_op jit(solution)/shard_map/slice | solution.py:106
  218.2 12.8 %collective-permute-done.2 = bf16[3,64,3584]{2,1,0:T(8,128)(2,1)} collective-permute-done((bf16[3,64,3584]{2,1,0:T(8,128)(2,1)}, bf16[3,64,3584]{2,1,0:T(8,128)(2,1)}, u32[]{:S(2)}, u32[]{:S(2)}) %collective-permute-start.2) | collective-permute-done | bytes 1376288 | tf_op jit(solution)/shard_map/ppermute | solution.py:32
  231.0 2.9 multiply_convert_fusion.5
  236.4 6.6 %bitcast_add_fusion.6 = (f32[128,3584]{1,0:T(8,128)}, f32[128,3584]{1,0:T(8,128)}, f32[128,3584]{1,0:T(8,128)S(1)}) fusion(f32[128,3584]{1,0:T(8,128)S(1)} %copy-done.16, f32[3,128,3584]{2,1,0:T(8,128)} %collective-permute-done.6, f32[128,3584]{1,0:T(8,128)S(1)} %copy-done.17, f32[128,3584]{1,0:T(8,128)} %get-tuple-element.94), kind=kLoop, calls=%fused_computation.69 | loop fusion | flops 1376256 | bytes 16515072 | tf_op jit(solution)/shard_map/add | solution.py:121
  249.6 5.8 fusion.100
  255.4 4.0 fusion.99
  267.3 7.6 %fusion.101 = f32[256,3584]{1,0:T(8,128)S(1)} fusion(bf16[256,2048]{0,1:T(8,128)(2,1)S(1)} %bitcast.303, bf16[3584,2048]{1,0:T(8,128)(2,1)} %param.9), kind=kOutput, calls=%fused_computation.301 | convolution fusion | flops 3758096384 | bytes 19398656 | tf_op jit(solution)/shard_map/dot_general | solution.py:19
  282.2 2.8 pad_maximum_fusion.2
  290.2 2.6 slice_bitcast_fusion.24
  292.8 9.0 %fusion.4 = f32[256,2048]{1,0:T(8,128)} fusion(bf16[2048,3584]{1,0:T(8,128)(2,1)} %param.7, bf16[128,3584]{1,0:T(8,128)(2,1)S(1)} %get-tuple-element.258, bf16[128,3584]{1,0:T(8,128)(2,1)S(1)} %get-tuple-element.256), kind=kOutput, calls=%fused_computation.32 | convolution fusion | flops 3761766400 | bytes 18612224 | tf_op jit(solution)/shard_map/dot_general | solution.py:19
  301.8 11.3 %fusion = bf16[256,2048]{1,0:T(8,128)(2,1)} fusion(f32[256,2048]{1,0:T(8,128)} %fusion.4, bf16[2048,3584]{1,0:T(8,128)(2,1)} %param.8, bf16[128,3584]{1,0:T(8,128)(2,1)} %get-tuple-element.257, bf16[128,3584]{1,0:T(8,128)(2,1)} %get-tuple-element.255), kind=kOutput, calls=%fused_computation.11 | convolution fusion | flops 3762814976 | bytes 19660800 | tf_op jit(solution)/shard_map/dot_general | solution.py:19
  322.1 2.8 constant_dynamic-update-slice_fusion.6
  325.0 7.3 %bitcast_add_fusion.3 = (f32[128,3584]{1,0:T(8,128)}, f32[128,3584]{1,0:T(8,128)}, f32[128,3584]{1,0:T(8,128)}) fusion(f32[128,3584]{1,0:T(8,128)} %get-tuple-element.113, f32[3,128,3584]{2,1,0:T(8,128)} %collective-permute-done.12, f32[128,3584]{1,0:T(8,128)} %get-tuple-element.112, f32[128,3584]{1,0:T(8,128)} %get-tuple-element.110), kind=kLoop, calls=%fused_computation.66 | loop fusion | flops 1376256 | bytes 16515072 | tf_op jit(solution)/shard_map/add | solution.py:121
  339.0 6.1 %fusion.103 = f32[256,3584]{1,0:T(8,128)} fusion(bf16[256,2048]{0,1:T(8,128)(2,1)S(1)} %bitcast.282, bf16[2048,3584]{1,0:T(8,128)(2,1)S(1)} %bitcast.269), kind=kOutput, calls=%fused_computation.303 | convolution fusion | flops 3758096384 | bytes 19398656 | tf_op jit(solution)/shard_map/dot_general | solution.py:111
  345.2 4.0 fusion.102
  356.6 11.4 %fusion.104 = f32[256,3584]{1,0:T(8,128)} fusion(bf16[256,2048]{0,1:T(8,128)(2,1)} %bitcast.302, bf16[3584,2048]{1,0:T(8,128)(2,1)} %param.9), kind=kOutput, calls=%fused_computation.304 | convolution fusion | flops 3758096384 | bytes 19398656 | tf_op jit(solution)/shard_map/dot_general | solution.py:19
  367.9 3.7 slice_bitcast_fusion
  371.7 2.8 pad_maximum_fusion.3
  377.2 8.6 %fusion.11 = f32[256,2048]{1,0:T(8,128)} fusion(bf16[2048,3584]{1,0:T(8,128)(2,1)} %param.7, bf16[128,3584]{1,0:T(8,128)(2,1)S(1)} %get-tuple-element.252, bf16[128,3584]{1,0:T(8,128)(2,1)S(1)} %get-tuple-element.250), kind=kOutput, calls=%fused_computation.40 | convolution fusion | flops 3761766400 | bytes 18612224 | tf_op jit(solution)/shard_map/dot_general | solution.py:19
  385.9 11.3 %fusion.1 = bf16[256,2048]{1,0:T(8,128)(2,1)} fusion(f32[256,2048]{1,0:T(8,128)} %fusion.11, bf16[2048,3584]{1,0:T(8,128)(2,1)} %param.8, bf16[128,3584]{1,0:T(8,128)(2,1)} %get-tuple-element.251, bf16[128,3584]{1,0:T(8,128)(2,1)} %get-tuple-element.249), kind=kOutput, calls=%fused_computation.12 | convolution fusion | flops 3762814976 | bytes 19660800 | tf_op jit(solution)/shard_map/dot_general | solution.py:19
  410.4 18.7 %collective-permute-done.18 = bf16[2,64,3584]{2,1,0:T(8,128)(2,1)S(1)} collective-permute-done((bf16[2,64,3584]{2,1,0:T(8,128)(2,1)S(1)}, bf16[2,64,3584]{2,1,0:T(8,128)(2,1)S(1)}, u32[]{:S(2)}, u32[]{:S(2)}) %collective-permute-start.18) | collective-permute-done | bytes 917536 | tf_op jit(solution)/shard_map/ppermute | solution.py:32
  431.7 3.5 bitcast_add_fusion
  443.2 8.6 %fusion.18 = f32[256,2048]{1,0:T(8,128)} fusion(bf16[2048,3584]{1,0:T(8,128)(2,1)} %param.7, bf16[128,3584]{1,0:T(8,128)(2,1)S(1)} %get-tuple-element.246, bf16[128,3584]{1,0:T(8,128)(2,1)S(1)} %get-tuple-element.244), kind=kOutput, calls=%fused_computation.48 | convolution fusion | flops 3761766400 | bytes 18612224 | tf_op jit(solution)/shard_map/dot_general | solution.py:19
  451.8 11.3 %fusion.2 = bf16[256,2048]{1,0:T(8,128)(2,1)} fusion(f32[256,2048]{1,0:T(8,128)} %fusion.18, bf16[2048,3584]{1,0:T(8,128)(2,1)} %param.8, bf16[128,3584]{1,0:T(8,128)(2,1)} %get-tuple-element.245, bf16[128,3584]{1,0:T(8,128)(2,1)} %get-tuple-element.243), kind=kOutput, calls=%fused_computation.13 | convolution fusion | flops 3762814976 | bytes 19660800 | tf_op jit(solution)/shard_map/dot_general | solution.py:19
  463.1 2.4 fusion.92
  465.6 7.0 %collective-permute-done.25 = bf16[3,64,3584]{2,1,0:T(8,128)(2,1)} collective-permute-done((bf16[3,64,3584]{2,1,0:T(8,128)(2,1)}, bf16[3,64,3584]{2,1,0:T(8,128)(2,1)}, u32[]{:S(2)}, u32[]{:S(2)}) %collective-permute-start.25) | collective-permute-done | bytes 1376288 | tf_op jit(solution)/shard_map/ppermute | solution.py:32
  486.7 10.2 %collective-permute-done.26 = bf16[2,64,3584]{2,1,0:T(8,128)(2,1)S(1)} collective-permute-done((bf16[2,64,3584]{2,1,0:T(8,128)(2,1)S(1)}, bf16[2,64,3584]{2,1,0:T(8,128)(2,1)S(1)}, u32[]{:S(2)}, u32[]{:S(2)}) %collective-permute-start.26) | collective-permute-done | bytes 917536 | tf_op jit(solution)/shard_map/ppermute | solution.py:32
  503.7 8.6 %fusion.25 = f32[256,2048]{1,0:T(8,128)} fusion(bf16[2048,3584]{1,0:T(8,128)(2,1)} %param.7, bf16[128,3584]{1,0:T(8,128)(2,1)S(1)} %get-tuple-element.240, bf16[128,3584]{1,0:T(8,128)(2,1)S(1)} %get-tuple-element.238), kind=kOutput, calls=%fused_computation.56 | convolution fusion | flops 3761766400 | bytes 18612224 | tf_op jit(solution)/shard_map/dot_general | solution.py:19
  512.3 11.4 %fusion.3 = bf16[256,2048]{1,0:T(8,128)(2,1)} fusion(f32[256,2048]{1,0:T(8,128)} %fusion.25, bf16[2048,3584]{1,0:T(8,128)(2,1)} %param.8, bf16[128,3584]{1,0:T(8,128)(2,1)} %get-tuple-element.239, bf16[128,3584]{1,0:T(8,128)(2,1)} %get-tuple-element.237), kind=kOutput, calls=%fused_computation.14 | convolution fusion | flops 3762814976 | bytes 19660800 | tf_op jit(solution)/shard_map/dot_general | solution.py:19
  534.5 20.8 %multiply_convert_fusion.1 = bf16[2048,3584]{1,0:T(8,128)(2,1)} fusion(bf16[1024,3584]{1,0:T(8,128)(2,1)} %get-tuple-element.151, bf16[256,2048]{0,1:T(8,128)(2,1)S(1)} %bitcast.284, bf16[256,2048]{0,1:T(8,128)(2,1)S(1)} %bitcast.280, bf16[256,2048]{0,1:T(8,128)(2,1)S(1)} %bitcast.276, bf16[256,2048]{0,1:T(8,128)(2,1)S(1)} %bitcast.272), kind=kOutput, calls=%fused_computation.1 | convolution fusion | flops 15063842816 | bytes 26214400 | tf_op jit(solution)/shard_map/dot_general | solution.py:25
  559.2 2.9 collective-permute-start.35
  564.3 20.8 %multiply_convert_fusion = bf16[2048,3584]{1,0:T(8,128)(2,1)} fusion(bf16[1024,3584]{1,0:T(8,128)(2,1)} %get-tuple-element.156, bf16[256,2048]{0,1:T(8,128)(2,1)S(1)} %bitcast.285, bf16[256,2048]{0,1:T(8,128)(2,1)S(1)} %bitcast.281, bf16[256,2048]{0,1:T(8,128)(2,1)S(1)} %bitcast.277, bf16[256,2048]{0,1:T(8,128)(2,1)S(1)} %bitcast.273), kind=kOutput, calls=%fused_computation | convolution fusion | flops 15063842816 | bytes 26214400 | tf_op jit(solution)/shard_map/dot_general | solution.py:25
  586.5 8.6 %collective-permute-done.34 = bf16[128,1024]{1,0:T(8,128)(2,1)} collective-permute-done((bf16[128,1024]{1,0:T(8,128)(2,1)}, bf16[128,1024]{1,0:T(8,128)(2,1)}, u32[]{:S(2)}, u32[]{:S(2)}) %collective-permute-start.34) | collective-permute-done | bytes 262176 | tf_op jit(solution)/shard_map/ppermute | solution.py:32
  (344 shorter events, 160.9 us)
Async XLA Ops:
  7.2 52.3 %all-gather.9.cloned.1.call-start = ((), (), s32[]{:S(2)}) async-start(), calls=%async_computation | async-start | bytes 2621440 | tf_op jit(solution)/shard_map/all_gather | solution.py:99
  10.7 126.8 %all-gather.11.cloned.1.call-start = ((), (), s32[]{:S(2)}) async-start(), calls=%async_computation.1 | async-start | bytes 2621440 | tf_op jit(solution)/shard_map/all_gather | solution.py:99
  61.2 2.7 collective-permute-start
  91.6 57.9 %collective-permute-start.1 = (f32[3,128,3584]{2,1,0:T(8,128)}, f32[3,128,3584]{2,1,0:T(8,128)}, u32[]{:S(2)}, u32[]{:S(2)}) collective-permute-start(f32[3,128,3584]{2,1,0:T(8,128)} %pad_maximum_fusion), channel_id=1, source_target_pairs={{0,2},{2,0},{1,3},{3,1},{4,6},{6,4},{5,7},{7,5},{8,10},{10,8},{9,1... | collective-permute-start | bytes 16515080 | tf_op jit(solution)/shard_map/ppermute | solution.py:32
  92.7 98.6 %all-gather.13.cloned.1.call-start = ((), (), s32[]{:S(2)}) async-start(), calls=%async_computation.2 | async-start | bytes 2621440 | tf_op jit(solution)/shard_map/all_gather | solution.py:99
  140.3 3.0 collective-permute-start.3
  141.2 135.8 %all-gather.15.cloned.1.call-start = ((), (), s32[]{:S(2)}) async-start(), calls=%async_computation.3 | async-start | bytes 2621440 | tf_op jit(solution)/shard_map/all_gather | solution.py:99
  191.0 45.4 %collective-permute-start.6 = (f32[3,128,3584]{2,1,0:T(8,128)}, f32[3,128,3584]{2,1,0:T(8,128)}, u32[]{:S(2)}, u32[]{:S(2)}) collective-permute-start(f32[3,128,3584]{2,1,0:T(8,128)} %pad_maximum_fusion.1), channel_id=1, source_target_pairs={{0,2},{2,0},{1,3},{3,1},{4,6},{6,4},{5,7},{7,5},{8,10},{10,8},{9,1... | collective-permute-start | bytes 16515080 | tf_op jit(solution)/shard_map/ppermute | solution.py:32
  193.0 8.6 %collective-permute-start.5 = (bf16[2,2,128,1024]{3,2,1,0:T(8,128)(2,1)S(1)}, bf16[2,2,128,1024]{3,2,1,0:T(8,128)(2,1)}, u32[]{:S(2)}, u32[]{:S(2)}) collective-permute-start(bf16[2,2,128,1024]{3,2,1,0:T(8,128)(2,1)S(1)} %get-tuple-element.212), channel_id=1, source_target_pairs={{0,2},{2,0},{1,3},{3,1},{4,6},{6,4},{5,7},{7,5},{8,10},{10,8},{9,1... | collective-permute-start | bytes 3145736 | tf_op jit(solution)/shard_map/ppermute | solution.py:32
  198.4 32.6 %collective-permute-start.2 = (bf16[3,64,3584]{2,1,0:T(8,128)(2,1)}, bf16[3,64,3584]{2,1,0:T(8,128)(2,1)}, u32[]{:S(2)}, u32[]{:S(2)}) collective-permute-start(bf16[3,64,3584]{2,1,0:T(8,128)(2,1)} %pad_maximum_fusion.9), channel_id=1, source_target_pairs={{0,1},{1,0},{2,3},{3,2},{4,5},{5,4},{6,7},{7,6},{8,9},{9,8},{10,11... | collective-permute-start | bytes 4128776 | tf_op jit(solution)/shard_map/ppermute | solution.py:32
  205.6 30.8 %copy-start.17 = (f32[128,3584]{1,0:T(8,128)S(1)}, f32[128,3584]{1,0:T(8,128)}, u32[]{:S(2)}) copy-start(f32[128,3584]{1,0:T(8,128)} %get-tuple-element.96) | copy-start | bytes 5505028
  218.2 37.2 %copy-start.8 = (bf16[1,256,2,1024]{1,3,2,0:T(8,128)(2,1)}, bf16[1,256,2,1024]{1,3,2,0:T(8,128)(2,1)S(1)}, u32[]{:S(2)}) copy-start(bf16[1,256,2,1024]{1,3,2,0:T(8,128)(2,1)S(1)} %copy.20) | copy-start | bytes 3145732
  235.0 26.6 %collective-permute-start.4 = (bf16[2,64,3584]{2,1,0:T(8,128)(2,1)}, bf16[2,64,3584]{2,1,0:T(8,128)(2,1)}, u32[]{:S(2)}, u32[]{:S(2)}) collective-permute-start(bf16[2,64,3584]{2,1,0:T(8,128)(2,1)} %pad_maximum_fusion.14), channel_id=1, source_target_pairs={{0,1},{1,0},{2,3},{3,2},{4,5},{5,4},{6,7},{7,6},{8,9},{9,8},{10,11... | collective-permute-start | bytes 2752520 | tf_op jit(solution)/shard_map/ppermute | solution.py:32
  263.3 25.9 %collective-permute-start.7 = (bf16[2,128,3584]{2,1,0:T(8,128)(2,1)S(1)}, bf16[2,128,3584]{2,1,0:T(8,128)(2,1)}, u32[]{:S(2)}, u32[]{:S(2)}) collective-permute-start(bf16[2,128,3584]{2,1,0:T(8,128)(2,1)S(1)} %pad_maximum_fusion.5), channel_id=1, source_target_pairs={{0,2},{2,0},{1,3},{3,1},{4,6},{6,4},{5,7},{7,5},{8,10},{10,8},{9,1... | collective-permute-start | bytes 5505032 | tf_op jit(solution)/shard_map/ppermute | solution.py:32
  278.9 6.2 %collective-permute-start.11 = (bf16[2,2,128,1024]{3,2,1,0:T(8,128)(2,1)S(1)}, bf16[2,2,128,1024]{3,2,1,0:T(8,128)(2,1)S(1)}, u32[]{:S(2)}, u32[]{:S(2)}) collective-permute-start(bf16[2,2,128,1024]{3,2,1,0:T(8,128)(2,1)S(1)} %get-tuple-element.208), channel_id=1, source_target_pairs={{0,2},{2,0},{1,3},{3,1},{4,6},{6,4},{5,7},{7,5},{8,10},{10,8},{9,1... | collective-permute-start | bytes 3145736 | tf_op jit(solution)/shard_map/ppermute | solution.py:32
  281.6 33.9 %collective-permute-start.9 = (bf16[3,64,3584]{2,1,0:T(8,128)(2,1)}, bf16[3,64,3584]{2,1,0:T(8,128)(2,1)}, u32[]{:S(2)}, u32[]{:S(2)}) collective-permute-start(bf16[3,64,3584]{2,1,0:T(8,128)(2,1)} %pad_maximum_fusion.10), channel_id=1, source_target_pairs={{0,1},{1,0},{2,3},{3,2},{4,5},{5,4},{6,7},{7,6},{8,9},{9,8},{10,11... | collective-permute-start | bytes 4128776 | tf_op jit(solution)/shard_map/ppermute | solution.py:32
  285.0 40.0 %collective-permute-start.12 = (f32[3,128,3584]{2,1,0:T(8,128)}, f32[3,128,3584]{2,1,0:T(8,128)}, u32[]{:S(2)}, u32[]{:S(2)}) collective-permute-start(f32[3,128,3584]{2,1,0:T(8,128)} %pad_maximum_fusion.2), channel_id=1, source_target_pairs={{0,2},{2,0},{1,3},{3,1},{4,6},{6,4},{5,7},{7,5},{8,10},{10,8},{9,1... | collective-permute-start | bytes 16515080 | tf_op jit(solution)/shard_map/ppermute | solution.py:32
  315.5 83.8 %collective-permute-start.8 = (bf16[128,2048]{1,0:T(8,128)(2,1)}, bf16[128,2048]{1,0:T(8,128)(2,1)}, u32[]{:S(2)}, u32[]{:S(2)}) collective-permute-start(bf16[128,2048]{1,0:T(8,128)(2,1)} %get-tuple-element.269), channel_id=1, source_target_pairs={{0,2},{2,0},{1,3},{3,1},{4,6},{6,4},{5,7},{7,5},{8,10},{10,8},{9,1... | collective-permute-start | bytes 1572872 | tf_op jit(solution)/shard_map/ppermute | solution.py:32
  316.0 23.0 %slice-start.20 = ((s8[14680064]{0:T(1024)(128)(4,1)}), s8[4194304]{0:T(1024)(128)(4,1)S(1)}, s32[]{:S(2)}) async-start(s8[14680064]{0:T(1024)(128)(4,1)} %bitcast.268), calls=%async_computation.24 | async-start | bytes 8388608
  319.3 35.5 %collective-permute-start.10 = (bf16[2,64,3584]{2,1,0:T(8,128)(2,1)}, bf16[2,64,3584]{2,1,0:T(8,128)(2,1)}, u32[]{:S(2)}, u32[]{:S(2)}) collective-permute-start(bf16[2,64,3584]{2,1,0:T(8,128)(2,1)} %pad_maximum_fusion.15), channel_id=1, source_target_pairs={{0,1},{1,0},{2,3},{3,2},{4,5},{5,4},{6,7},{7,6},{8,9},{9,8},{10,11... | collective-permute-start | bytes 2752520 | tf_op jit(solution)/shard_map/ppermute | solution.py:32
  325.0 20.2 %slice-start.12 = ((s8[14680064]{0:T(1024)(128)(4,1)}), s8[4194304]{0:T(1024)(128)(4,1)S(1)}, s32[]{:S(2)}) async-start(s8[14680064]{0:T(1024)(128)(4,1)} %bitcast.264), calls=%async_computation.16 | async-start | bytes 8388608
  325.0 20.2 %slice-start.13 = ((s8[14680064]{0:T(1024)(128)(4,1)}), s8[2097152]{0:T(1024)(128)(4,1)S(1)}, s32[]{:S(2)}) async-start(s8[14680064]{0:T(1024)(128)(4,1)} %bitcast.264), calls=%async_computation.17 | async-start | bytes 4194304
  350.4 48.9 %collective-permute-start.17 = (bf16[3,64,3584]{2,1,0:T(8,128)(2,1)}, bf16[3,64,3584]{2,1,0:T(8,128)(2,1)}, u32[]{:S(2)}, u32[]{:S(2)}) collective-permute-start(bf16[3,64,3584]{2,1,0:T(8,128)(2,1)} %pad_maximum_fusion.11), channel_id=1, source_target_pairs={{0,1},{1,0},{2,3},{3,2},{4,5},{5,4},{6,7},{7,6},{8,9},{9,8},{10,11... | collective-permute-start | bytes 4128776 | tf_op jit(solution)/shard_map/ppermute | solution.py:32
  356.5 18.5 %collective-permute-start.13 = (bf16[2,128,3584]{2,1,0:T(8,128)(2,1)S(1)}, bf16[2,128,3584]{2,1,0:T(8,128)(2,1)S(1)}, u32[]{:S(2)}, u32[]{:S(2)}) collective-permute-start(bf16[2,128,3584]{2,1,0:T(8,128)(2,1)S(1)} %pad_maximum_fusion.6), channel_id=1, source_target_pairs={{0,2},{2,0},{1,3},{3,1},{4,6},{6,4},{5,7},{7,5},{8,10},{10,8},{9,1... | collective-permute-start | bytes 5505032 | tf_op jit(solution)/shard_map/ppermute | solution.py:32
  374.5 54.8 %collective-permute-start.20 = (f32[3,128,3584]{2,1,0:T(8,128)}, f32[3,128,3584]{2,1,0:T(8,128)}, u32[]{:S(2)}, u32[]{:S(2)}) collective-permute-start(f32[3,128,3584]{2,1,0:T(8,128)} %pad_maximum_fusion.3), channel_id=1, source_target_pairs={{0,2},{2,0},{1,3},{3,1},{4,6},{6,4},{5,7},{7,5},{8,10},{10,8},{9,1... | collective-permute-start | bytes 16515080 | tf_op jit(solution)/shard_map/ppermute | solution.py:32
  402.1 75.6 %collective-permute-start.16 = (bf16[128,1024]{1,0:T(8,128)(2,1)}, bf16[128,1024]{1,0:T(8,128)(2,1)}, u32[]{:S(2)}, u32[]{:S(2)}) collective-permute-start(bf16[128,1024]{1,0:T(8,128)(2,1)} %get-tuple-element.263), channel_id=1, source_target_pairs={{0,12},{4,0},{8,4},{12,8},{1,13},{5,1},{9,5},{13,9},{2,14},{6,2},{... | collective-permute-start | bytes 786440 | tf_op jit(solution)/shard_map/ppermute | solution.py:32
  403.5 74.2 %collective-permute-start.14 = (bf16[128,1024]{1,0:T(8,128)(2,1)}, bf16[128,1024]{1,0:T(8,128)(2,1)}, u32[]{:S(2)}, u32[]{:S(2)}) collective-permute-start(bf16[128,1024]{1,0:T(8,128)(2,1)} %get-tuple-element.265), channel_id=1, source_target_pairs={{0,4},{4,8},{8,12},{12,0},{1,5},{5,9},{9,13},{13,1},{2,6},{6,10},{... | collective-permute-start | bytes 786440 | tf_op jit(solution)/shard_map/ppermute | solution.py:32
  404.3 73.4 %collective-permute-start.15 = (bf16[128,1024]{1,0:T(8,128)(2,1)}, bf16[128,1024]{1,0:T(8,128)(2,1)}, u32[]{:S(2)}, u32[]{:S(2)}) collective-permute-start(bf16[128,1024]{1,0:T(8,128)(2,1)} %get-tuple-element.266), channel_id=1, source_target_pairs={{0,8},{4,12},{8,0},{12,4},{1,9},{5,13},{9,1},{13,5},{2,10},{6,14},... | collective-permute-start | bytes 786440 | tf_op jit(solution)/shard_map/ppermute | solution.py:32
  407.5 21.5 %collective-permute-start.18 = (bf16[2,64,3584]{2,1,0:T(8,128)(2,1)S(1)}, bf16[2,64,3584]{2,1,0:T(8,128)(2,1)S(1)}, u32[]{:S(2)}, u32[]{:S(2)}) collective-permute-start(bf16[2,64,3584]{2,1,0:T(8,128)(2,1)S(1)} %pad_maximum_fusion.16), channel_id=1, source_target_pairs={{0,1},{1,0},{2,3},{3,2},{4,5},{5,4},{6,7},{7,6},{8,9},{9,8},{10,11... | collective-permute-start | bytes 2752520 | tf_op jit(solution)/shard_map/ppermute | solution.py:32
  429.0 48.7 %collective-permute-start.21 = (bf16[128,2048]{1,0:T(8,128)(2,1)}, bf16[128,2048]{1,0:T(8,128)(2,1)}, u32[]{:S(2)}, u32[]{:S(2)}) collective-permute-start(bf16[128,2048]{1,0:T(8,128)(2,1)} %get-tuple-element.277), channel_id=1, source_target_pairs={{0,2},{2,0},{1,3},{3,1},{4,6},{6,4},{5,7},{7,5},{8,10},{10,8},{9,1... | collective-permute-start | bytes 1572872 | tf_op jit(solution)/shard_map/ppermute | solution.py:32
  429.3 9.0 %collective-permute-start.19 = (bf16[2,128,3584]{2,1,0:T(8,128)(2,1)S(1)}, bf16[2,128,3584]{2,1,0:T(8,128)(2,1)S(1)}, u32[]{:S(2)}, u32[]{:S(2)}) collective-permute-start(bf16[2,128,3584]{2,1,0:T(8,128)(2,1)S(1)} %pad_maximum_fusion.7), channel_id=1, source_target_pairs={{0,2},{2,0},{1,3},{3,1},{4,6},{6,4},{5,7},{7,5},{8,10},{10,8},{9,1... | collective-permute-start | bytes 5505032 | tf_op jit(solution)/shard_map/ppermute | solution.py:32
  439.7 32.9 %collective-permute-start.25 = (bf16[3,64,3584]{2,1,0:T(8,128)(2,1)}, bf16[3,64,3584]{2,1,0:T(8,128)(2,1)}, u32[]{:S(2)}, u32[]{:S(2)}) collective-permute-start(bf16[3,64,3584]{2,1,0:T(8,128)(2,1)} %pad_maximum_fusion.12), channel_id=1, source_target_pairs={{0,1},{1,0},{2,3},{3,2},{4,5},{5,4},{6,7},{7,6},{8,9},{9,8},{10,11... | collective-permute-start | bytes 4128776 | tf_op jit(solution)/shard_map/ppermute | solution.py:32
  474.9 22.0 %collective-permute-start.26 = (bf16[2,64,3584]{2,1,0:T(8,128)(2,1)S(1)}, bf16[2,64,3584]{2,1,0:T(8,128)(2,1)S(1)}, u32[]{:S(2)}, u32[]{:S(2)}) collective-permute-start(bf16[2,64,3584]{2,1,0:T(8,128)(2,1)S(1)} %pad_maximum_fusion.17), channel_id=1, source_target_pairs={{0,1},{1,0},{2,3},{3,2},{4,5},{5,4},{6,7},{7,6},{8,9},{9,8},{10,11... | collective-permute-start | bytes 2752520 | tf_op jit(solution)/shard_map/ppermute | solution.py:32
  480.4 77.3 %collective-permute-start.24 = (bf16[128,1024]{1,0:T(8,128)(2,1)}, bf16[128,1024]{1,0:T(8,128)(2,1)}, u32[]{:S(2)}, u32[]{:S(2)}) collective-permute-start(bf16[128,1024]{1,0:T(8,128)(2,1)} %get-tuple-element.271), channel_id=1, source_target_pairs={{0,12},{4,0},{8,4},{12,8},{1,13},{5,1},{9,5},{13,9},{2,14},{6,2},{... | collective-permute-start | bytes 786440 | tf_op jit(solution)/shard_map/ppermute | solution.py:32
  482.7 76.5 %collective-permute-start.22 = (bf16[128,1024]{1,0:T(8,128)(2,1)}, bf16[128,1024]{1,0:T(8,128)(2,1)}, u32[]{:S(2)}, u32[]{:S(2)}) collective-permute-start(bf16[128,1024]{1,0:T(8,128)(2,1)} %get-tuple-element.273), channel_id=1, source_target_pairs={{0,4},{4,8},{8,12},{12,0},{1,5},{5,9},{9,13},{13,1},{2,6},{6,10},{... | collective-permute-start | bytes 786440 | tf_op jit(solution)/shard_map/ppermute | solution.py:32
  483.2 79.0 %collective-permute-start.23 = (bf16[128,1024]{1,0:T(8,128)(2,1)}, bf16[128,1024]{1,0:T(8,128)(2,1)}, u32[]{:S(2)}, u32[]{:S(2)}) collective-permute-start(bf16[128,1024]{1,0:T(8,128)(2,1)} %get-tuple-element.274), channel_id=1, source_target_pairs={{0,8},{4,12},{8,0},{12,4},{1,9},{5,13},{9,1},{13,5},{2,10},{6,14},... | collective-permute-start | bytes 786440 | tf_op jit(solution)/shard_map/ppermute | solution.py:32
  484.7 44.5 %collective-permute-start.28 = (bf16[128,2048]{1,0:T(8,128)(2,1)}, bf16[128,2048]{1,0:T(8,128)(2,1)}, u32[]{:S(2)}, u32[]{:S(2)}) collective-permute-start(bf16[128,2048]{1,0:T(8,128)(2,1)} %get-tuple-element.285), channel_id=1, source_target_pairs={{0,2},{2,0},{1,3},{3,1},{4,6},{6,4},{5,7},{7,5},{8,10},{10,8},{9,1... | collective-permute-start | bytes 1572872 | tf_op jit(solution)/shard_map/ppermute | solution.py:32
  497.2 4.3 collective-permute-start.27
  524.8 3.5 collective-permute-start.32
  532.0 30.4 %collective-permute-start.31 = (bf16[128,1024]{1,0:T(8,128)(2,1)}, bf16[128,1024]{1,0:T(8,128)(2,1)S(1)}, u32[]{:S(2)}, u32[]{:S(2)}) collective-permute-start(bf16[128,1024]{1,0:T(8,128)(2,1)} %get-tuple-element.279), channel_id=1, source_target_pairs={{0,12},{4,0},{8,4},{12,8},{1,13},{5,1},{9,5},{13,9},{2,14},{6,2},{... | collective-permute-start | bytes 786440 | tf_op jit(solution)/shard_map/ppermute | solution.py:32
  534.2 52.3 %collective-permute-start.29 = (bf16[128,1024]{1,0:T(8,128)(2,1)}, bf16[128,1024]{1,0:T(8,128)(2,1)}, u32[]{:S(2)}, u32[]{:S(2)}) collective-permute-start(bf16[128,1024]{1,0:T(8,128)(2,1)} %get-tuple-element.281), channel_id=1, source_target_pairs={{0,4},{4,8},{8,12},{12,0},{1,5},{5,9},{9,13},{13,1},{2,6},{6,10},{... | collective-permute-start | bytes 786440 | tf_op jit(solution)/shard_map/ppermute | solution.py:32
  557.7 28.8 %collective-permute-start.30 = (bf16[128,1024]{1,0:T(8,128)(2,1)}, bf16[128,1024]{1,0:T(8,128)(2,1)}, u32[]{:S(2)}, u32[]{:S(2)}) collective-permute-start(bf16[128,1024]{1,0:T(8,128)(2,1)} %get-tuple-element.282), channel_id=1, source_target_pairs={{0,8},{4,12},{8,0},{12,4},{1,9},{5,13},{9,1},{13,5},{2,10},{6,14},... | collective-permute-start | bytes 786440 | tf_op jit(solution)/shard_map/ppermute | solution.py:32
  559.2 27.3 %collective-permute-start.35 = (bf16[128,1024]{1,0:T(8,128)(2,1)}, bf16[128,1024]{1,0:T(8,128)(2,1)}, u32[]{:S(2)}, u32[]{:S(2)}) collective-permute-start(bf16[128,1024]{1,0:T(8,128)(2,1)} %get-tuple-element.288), channel_id=1, source_target_pairs={{0,12},{4,0},{8,4},{12,8},{1,13},{5,1},{9,5},{13,9},{2,14},{6,2},{... | collective-permute-start | bytes 786440 | tf_op jit(solution)/shard_map/ppermute | solution.py:32
  562.1 24.4 %collective-permute-start.33 = (bf16[128,1024]{1,0:T(8,128)(2,1)}, bf16[128,1024]{1,0:T(8,128)(2,1)}, u32[]{:S(2)}, u32[]{:S(2)}) collective-permute-start(bf16[128,1024]{1,0:T(8,128)(2,1)} %get-tuple-element.290), channel_id=1, source_target_pairs={{0,4},{4,8},{8,12},{12,0},{1,5},{5,9},{9,13},{13,1},{2,6},{6,10},{... | collective-permute-start | bytes 786440 | tf_op jit(solution)/shard_map/ppermute | solution.py:32
  563.1 22.0 %copy-start.41 = (bf16[128,1024]{1,0:T(8,128)(2,1)S(1)}, bf16[128,1024]{1,0:T(8,128)(2,1)}, u32[]{:S(2)}) copy-start(bf16[128,1024]{1,0:T(8,128)(2,1)} %get-tuple-element.145) | copy-start | bytes 786436
  563.1 32.0 %copy-start.43 = (bf16[128,1024]{1,0:T(8,128)(2,1)S(1)}, bf16[128,1024]{1,0:T(8,128)(2,1)}, u32[]{:S(2)}) copy-start(bf16[128,1024]{1,0:T(8,128)(2,1)} %get-tuple-element.152) | copy-start | bytes 786436
  563.1 32.0 %copy-start.54 = (bf16[128,1024]{1,0:T(8,128)(2,1)S(1)}, bf16[128,1024]{1,0:T(8,128)(2,1)}, u32[]{:S(2)}) copy-start(bf16[128,1024]{1,0:T(8,128)(2,1)} %copy-done.53) | copy-start | bytes 786436
  563.1 32.0 %collective-permute-start.34 = (bf16[128,1024]{1,0:T(8,128)(2,1)}, bf16[128,1024]{1,0:T(8,128)(2,1)}, u32[]{:S(2)}, u32[]{:S(2)}) collective-permute-start(bf16[128,1024]{1,0:T(8,128)(2,1)} %get-tuple-element.291), channel_id=1, source_target_pairs={{0,8},{4,12},{8,0},{12,4},{1,9},{5,13},{9,1},{13,5},{2,10},{6,14},... | collective-permute-start | bytes 786440 | tf_op jit(solution)/shard_map/ppermute | solution.py:32
  (71 other events, 467.3 us)
Sparse Core Ops, SparseCore 0:
  10.8 48.6 all-gather.8
  92.8 44.6 all-gather.10
  141.3 44.7 all-gather.12
  200.9 44.0 all-gather.14
